TPU v7x, 128 devices: a whole 4x4x4 slice. The times are simulated.
128 devices in a mesh: slit: 16 (over x, y_hi, core), span: 8 (over z, y_lo).
Axes of the slice: x: 4, y: 4 (y_hi: 2, y_lo: 2; y = y_hi * 2 + y_lo), z: 4, core: 2. Of those that a mesh axis runs over, the one named last changes fastest.
Arguments:
- query_tiles: bfloat16 [64, 16, 128, 768], P('slit', 'span'), may hold values from -4 to 4
- key_tiles: bfloat16 [64, 16, 128, 768], P('slit', 'span'), may hold values from -4 to 4
- value_tiles: bfloat16 [64, 16, 128, 768], P('slit', 'span'), may hold values from -3 to 3
- forward_out: bfloat16 [64, 16, 128, 768], P('slit', 'span'), may hold values from -3 to 3
- out_grad: bfloat16 [64, 16, 128, 768], P('slit', 'span'), may hold values from -3 to 3
- row_lse: float32 [64, 16, 12, 128], P('slit', 'span'), may hold values from 2 to 3.5
- neighbours: int32 [64, 16, 8], P('slit', 'span'), may hold values from 0 to 1023, as said below
- flags: int32 [64, 16, 8], P('slit', 'span'), may hold values from 0 to 1
Outputs:
- query_grad: bfloat16 [64, 16, 128, 768], P('slit', 'span')
- key_grad: bfloat16 [64, 16, 128, 768], P('slit', 'span')
- value_grad: bfloat16 [64, 16, 128, 768], P('slit', 'span')
Inputs may be any that keep to these rules, and one draw needn't show every extreme that they name: `neighbours`: every listed key block lies within one block of its query block along both directions (slit positions taken modulo 64, transverse positions not wrapped); the entries with flag 1 come first in each list, are distinct, number at least 1, and some query block has all 8 entries used; padded entries hold the query block's own id.
All inputs are finite; a program needn't handle non-finite values.
Results may differ from a plain program's by a relative error of at most 0.006.
Values may be sent and summed in bfloat16 or wider, within the bound.
No kernel may reach another device: no remote copies, remote signals or barrier semaphores. Data moves between devices by JAX's collectives and lax.ppermute only.
A program may use at most 192 MiB of HBM per device.

v0:
```python
import math

import jax
import jax.numpy as jnp
from jax import lax
from jax.sharding import PartitionSpec as P


def from_behind(x, axis, by):
    size = lax.axis_size(axis)
    pairs = [(i, i + by) for i in range(size) if 0 <= i + by < size]
    return lax.ppermute(x, axis, pairs)


def from_behind_2(x, axis, by):
    size = lax.axis_size(axis)
    return lax.ppermute(x, axis, [(i, (i + by) % size) for i in range(size)])


def extended(cells, sides, width):
    for axis, dim in sides:
        count = lax.axis_size(axis)
        head = lax.slice_in_dim(cells, 0, width, axis=dim)
        tail = lax.slice_in_dim(cells, cells.shape[dim] - width, cells.shape[dim], axis=dim)
        cells = jnp.concatenate(
            [
                lax.ppermute(tail, axis, [(i, (i + 1) % count) for i in range(count)]),
                cells,
                lax.ppermute(head, axis, [((i + 1) % count, i) for i in range(count)]),
            ],
            axis=dim,
        )
    return cells


def fold_back(padded):
    rows_a = padded.shape[0] - 2
    rows_b = padded.shape[1] - 2
    from_lower = from_behind(padded[:, rows_b + 1 : rows_b + 2], "span", 1)
    from_upper = from_behind(padded[:, 0:1], "span", -1)
    middle = padded[:, 1 : rows_b + 1]
    middle = middle.at[:, 0:1].add(from_lower)
    middle = middle.at[:, rows_b - 1 : rows_b].add(from_upper)
    from_left = from_behind_2(
        middle[rows_a + 1 : rows_a + 2].astype(jnp.bfloat16), "slit", 1
    ).astype(jnp.float32)
    from_right = from_behind_2(middle[0:1], "slit", -1)
    interior = middle[1 : rows_a + 1]
    interior = interior.at[0:1].add(from_left)
    interior = interior.at[rows_a - 1 : rows_a].add(from_right)
    return interior


def on_device(
    query_tiles, key_tiles, value_tiles, forward_out, out_grad, row_lse, neighbours, flags
):
    rows_a = query_tiles.shape[0]
    rows_b = query_tiles.shape[1]
    blk_len = query_tiles.shape[2]
    width = query_tiles.shape[3]
    heads = row_lse.shape[2]
    head_dim = width // heads
    list_len = neighbours.shape[2]
    factor = 1.0 / math.sqrt(head_dim)
    grid_a = rows_a * lax.axis_size("slit")
    grid_b = rows_b * lax.axis_size("span")
    base_a = lax.axis_index("slit") * rows_a
    base_b = lax.axis_index("span") * rows_b
    padded_count = (rows_a + 2) * (rows_b + 2)
    local_count = rows_a * rows_b
    split_shape = (rows_a, rows_b, blk_len, heads, head_dim)
    delta = jnp.einsum(
        "abthd,abthd->abht",
        out_grad.reshape(split_shape),
        forward_out.reshape(split_shape),
        preferred_element_type=jnp.float32,
    )
    out_shape = (rows_a, rows_b, blk_len, width)
    target_a = neighbours // grid_b
    target_b = neighbours % grid_b
    pad_a = (target_a - base_a + 1) % grid_a
    pad_b = target_b - base_b + 1
    slots = (pad_a * (rows_b + 2) + pad_b).reshape(local_count, list_len)
    masks = flags.reshape(local_count, list_len).astype(jnp.float32)
    query_items = (
        query_tiles.reshape(local_count, blk_len, heads, head_dim),
        out_grad.reshape(local_count, blk_len, heads, head_dim),
        row_lse.reshape(local_count, heads, blk_len),
        delta.reshape(local_count, heads, blk_len),
        slots,
        masks,
    )
    key_pad, value_pad = (
        extended(key_tiles, (("slit", 0), ("span", 1)), 1),
        extended(value_tiles, (("slit", 0), ("span", 1)), 1),
    )
    key_flat = key_pad.reshape(padded_count, blk_len, heads, head_dim)
    value_flat = value_pad.reshape(padded_count, blk_len, heads, head_dim)

    def per_query(running, item):
        query_blk, grad_blk, lse_blk, delta_blk, slot_row, mask_row = item
        key_sel = key_flat[slot_row]
        value_sel = value_flat[slot_row]
        scores = (
            jnp.einsum("thd,muhd->htmu", query_blk, key_sel, preferred_element_type=jnp.float32)
            * factor
        )
        probs = jnp.exp(scores - lse_blk[:, :, None, None]) * mask_row[None, None, :, None]
        probs_low = probs.astype(jnp.bfloat16)
        value_part = jnp.einsum(
            "htmu,thd->muhd", probs_low, grad_blk, preferred_element_type=jnp.float32
        )
        prob_grad = jnp.einsum(
            "thd,muhd->htmu", grad_blk, value_sel, preferred_element_type=jnp.float32
        )
        score_grad = (probs * (prob_grad - delta_blk[:, :, None, None])).astype(jnp.bfloat16)
        query_part = (
            jnp.einsum("htmu,muhd->thd", score_grad, key_sel, preferred_element_type=jnp.float32)
            * factor
        )
        key_part = (
            jnp.einsum("htmu,thd->muhd", score_grad, query_blk, preferred_element_type=jnp.float32)
            * factor
        )
        running = running.at[slot_row, 0].add(key_part)
        running = running.at[slot_row, 1].add(value_part)
        return (running, query_part.astype(jnp.bfloat16))

    start_acc = jnp.zeros((padded_count, 2, blk_len, heads, head_dim), jnp.float32)
    partial_acc, query_parts = lax.scan(per_query, start_acc, query_items)
    summed = fold_back(partial_acc.reshape(rows_a + 2, rows_b + 2, 2, blk_len, width))
    query_grad = query_parts.reshape(out_shape)
    key_grad = summed[:, :, 0].astype(jnp.bfloat16)
    value_grad = summed[:, :, 1].astype(jnp.bfloat16)
    return (query_grad, key_grad, value_grad)


def solution(mesh):
    in_specs = (
        P("slit", "span", None, None),
        P("slit", "span", None, None),
        P("slit", "span", None, None),
        P("slit", "span", None, None),
        P("slit", "span", None, None),
        P("slit", "span", None, None),
        P("slit", "span", None),
        P("slit", "span", None),
    )
    out_specs = (
        P("slit", "span", None, None),
        P("slit", "span", None, None),
        P("slit", "span", None, None),
    )
    return jax.shard_map(
        on_device, mesh=mesh, in_specs=in_specs, out_specs=out_specs, check_vma=False
    )
```

profile of v0, /device:TPU:71, one launch (start us, length us, event | category | flops | bytes accessed | tf_op | source)
XLA Modules:
  0.0 856.3 jit_solution(6870806045134648576)
XLA Ops:
  16.2 5.6 collective-permute-done.1
  44.7 9.1 %collective-permute-done.2 = bf16[6,1,128,768]{2,3,1,0:T(8,128)(2,1)} collective-permute-done((bf16[6,1,128,768]{2,3,1,0:T(8,128)(2,1)}, bf16[6,1,128,768]{2,3,1,0:T(8,128)(2,1)}, u32[]{:S(2)}, u32[]{:S(2)}) %collective-permute-start.2) | collective-permute-done | bytes 1179680 | tf_op jit(solution)/shard_map/ppermute | solution.py:27
  53.7 25.7 %collective-permute-done.3 = bf16[6,1,128,768]{2,3,1,0:T(8,128)(2,1)} collective-permute-done((bf16[6,1,128,768]{2,3,1,0:T(8,128)(2,1)}, bf16[6,1,128,768]{2,3,1,0:T(8,128)(2,1)}, u32[]{:S(2)}, u32[]{:S(2)}) %collective-permute-start.3) | collective-permute-done | bytes 1179680 | tf_op jit(solution)/shard_map/ppermute | solution.py:29
  79.5 4.8 pad_maximum_fusion
  84.3 13.8 %copy.37 = bf16[24,128,12,64]{3,2,1,0:T(8,128)(2,1)} copy(bf16[24,128,12,64]{1,3,2,0:T(8,128)(2,1)} %bitcast.117) | data formatting | bytes 9437184 | tf_op jit(solution)/shard_map/while | solution.py:130
  98.1 6.2 collective-permute-done.6
  104.3 22.3 %collective-permute-done.7 = bf16[6,1,128,768]{2,3,1,0:T(8,128)(2,1)} collective-permute-done((bf16[6,1,128,768]{2,3,1,0:T(8,128)(2,1)}, bf16[6,1,128,768]{2,3,1,0:T(8,128)(2,1)}, u32[]{:S(2)}, u32[]{:S(2)}) %collective-permute-start.7) | collective-permute-done | bytes 1179680 | tf_op jit(solution)/shard_map/ppermute | solution.py:29
  126.6 4.4 pad_maximum_fusion.1
  131.0 13.7 %copy.38 = bf16[24,128,12,64]{3,2,1,0:T(8,128)(2,1)} copy(bf16[24,128,12,64]{1,3,2,0:T(8,128)(2,1)} %bitcast.118) | data formatting | bytes 9437184 | tf_op jit(solution)/shard_map/while | solution.py:130
  144.8 8.9 %broadcast_in_dim.7 = f32[24,2,128,12,64]{2,4,3,1,0:T(8,128)} broadcast(f32[]{:T(128)} %constant.176.clone.1), dimensions={} | broadcast | bytes 18874372 | tf_op jit(solution)/shard_map/broadcast_in_dim | solution.py:129
  153.7 417.0 %while.16 = (s32[]{:T(128)}, f32[24,2,128,12,64]{2,4,3,1,0:T(8,128)}, bf16[8,128,12,64]{1,3,2,0:T(8,128)(2,1)}, s32[8,8]{1,0:T(8,128)S(1)}, bf16[8,128,12,64]{1,...) while((s32[]{:T(128)}, ...), condition=%wide.region_3.4_spmd, body=%wide.region_0.3_spmd.sunk | while | flops 1024918656 | bytes 100121304 | solution.py:130
  154.4 7.8 gather_fusion.1
  162.2 7.6 gather_fusion
  169.8 4.5 copy.64
  190.6 8.2 scatter_fusion
  198.9 6.9 scatter_fusion.1
  206.5 7.8 gather_fusion.1
  214.2 7.6 gather_fusion
  221.8 4.5 copy.64
  228.6 4.2 multiply_convert_fusion.2
  242.7 8.3 scatter_fusion
  251.0 6.9 scatter_fusion.1
  258.6 7.8 gather_fusion.1
  266.4 7.6 gather_fusion
  274.0 4.5 copy.64
  294.8 8.2 scatter_fusion
  303.0 6.8 scatter_fusion.1
  310.6 7.8 gather_fusion.1
  318.4 7.6 gather_fusion
  326.0 4.5 copy.64
  346.8 8.2 scatter_fusion
  355.1 7.0 scatter_fusion.1
  362.8 7.8 gather_fusion.1
  370.6 7.6 gather_fusion
  378.2 4.5 copy.64
  384.9 4.2 multiply_convert_fusion.2
  399.0 8.3 scatter_fusion
  407.3 7.0 scatter_fusion.1
  415.0 7.8 gather_fusion.1
  422.8 7.6 gather_fusion
  430.4 4.5 copy.64
  451.2 8.2 scatter_fusion
  459.5 6.9 scatter_fusion.1
  467.1 7.8 gather_fusion.1
  474.9 7.6 gather_fusion
  482.5 4.5 copy.64
  489.2 4.2 multiply_convert_fusion.2
  503.3 8.2 scatter_fusion
  511.6 6.9 scatter_fusion.1
  519.2 7.8 gather_fusion.1
  527.0 7.6 gather_fusion
  534.6 4.5 copy.64
  555.4 8.3 scatter_fusion
  563.7 7.0 scatter_fusion.1
  570.6 9.5 %fusion.42 = (f32[6,1,2,128,768]{3,4,2,1,0:T(8,128)}, f32[6,1,2,128,768]{3,4,2,1,0:T(8,128)}) fusion(f32[6,4,2,128,768]{3,4,2,1,0:T(8,128)} %bitcast.114), kind=kLoop, calls=%fused_computation.75 | loop fusion | bytes 18874368 | tf_op jit(solution)/shard_map/slice | solution.py:40
  580.1 4.3 collective-permute-start.8
  586.8 4.3 slice.225
  591.1 96.0 %collective-permute-done.8 = f32[6,1,2,128,768]{3,4,2,1,0:T(8,128)} collective-permute-done((f32[6,1,2,128,768]{3,4,2,1,0:T(8,128)}, f32[6,1,2,128,768]{3,4,2,1,0:T(8,128)}, u32[]{:S(2)}, u32[]{:S(2)}) %collective-permute-start.8) | collective-permute-done | bytes 4718624 | tf_op jit(solution)/shard_map/ppermute | solution.py:12
  687.1 5.2 fusion.34
  692.2 95.5 %collective-permute-done.9 = f32[6,1,2,128,768]{3,4,2,1,0:T(8,128)} collective-permute-done((f32[6,1,2,128,768]{3,4,2,1,0:T(8,128)}, f32[6,1,2,128,768]{3,4,2,1,0:T(8,128)}, u32[]{:S(2)}, u32[]{:S(2)}) %collective-permute-start.9) | collective-permute-done | bytes 4718624 | tf_op jit(solution)/shard_map/ppermute | solution.py:12
  787.7 6.4 fusion.33
  795.8 6.1 slice.230
  801.8 19.7 %collective-permute-done.10 = bf16[1,2,2,128,768]{3,4,2,1,0:T(8,128)(2,1)S(1)} collective-permute-done((bf16[1,2,2,128,768]{3,4,2,1,0:T(8,128)(2,1)S(1)}, bf16[1,2,2,128,768]{3,4,2,1,0:T(8,128)(2,1)S(1)}, u32[]{:S(2)}, u32[]{:S(2)}) %collective-permute-start.10) | collective-permute-done | bytes 786464 | tf_op jit(solution)/shard_map/ppermute | solution.py:17
  827.4 19.5 %collective-permute-done.11 = f32[1,2,2,128,768]{3,4,2,1,0:T(8,128)S(1)} collective-permute-done((f32[1,2,2,128,768]{3,4,2,1,0:T(8,128)S(1)}, f32[1,2,2,128,768]{3,4,2,1,0:T(8,128)S(1)}, u32[]{:S(2)}, u32[]{:S(2)}) %collective-permute-start.11) | collective-permute-done | bytes 1572896 | tf_op jit(solution)/shard_map/ppermute | solution.py:17
  (173 shorter events, 182.0 us)
Async XLA Ops:
  3.5 12.7 %collective-permute-start = (bf16[1,2,128,768]{2,3,1,0:T(8,128)(2,1)}, bf16[1,2,128,768]{2,3,1,0:T(8,128)(2,1)}, u32[]{:S(2)}, u32[]{:S(2)}) collective-permute-start(bf16[1,2,128,768]{2,3,1,0:T(8,128)(2,1)} %get-tuple-element.163), channel_id=1, source_target_pairs={{0,8},{8,16},{16,24},{24,32},{32,40},{40,48},{48,56},{56,64},{64,7... | collective-permute-start | bytes 1179656 | tf_op jit(solution)/shard_map/ppermute | solution.py:27
  7.0 14.9 %collective-permute-start.1 = (bf16[1,2,128,768]{2,3,1,0:T(8,128)(2,1)}, bf16[1,2,128,768]{2,3,1,0:T(8,128)(2,1)}, u32[]{:S(2)}, u32[]{:S(2)}) collective-permute-start(bf16[1,2,128,768]{2,3,1,0:T(8,128)(2,1)} %get-tuple-element.164), channel_id=1, source_target_pairs={{8,0},{16,8},{24,16},{32,24},{40,32},{48,40},{56,48},{64,56},{72,6... | collective-permute-start | bytes 1179656 | tf_op jit(solution)/shard_map/ppermute | solution.py:29
  8.9 18.2 %collective-permute-start.4 = (bf16[1,2,128,768]{2,3,1,0:T(8,128)(2,1)S(1)}, bf16[1,2,128,768]{2,3,1,0:T(8,128)(2,1)S(1)}, u32[]{:S(2)}, u32[]{:S(2)}) collective-permute-start(bf16[1,2,128,768]{2,3,1,0:T(8,128)(2,1)S(1)} %get-tuple-element.161), channel_id=1, source_target_pairs={{0,8},{8,16},{16,24},{24,32},{32,40},{40,48},{48,56},{56,64},{64,7... | collective-permute-start | bytes 1179656 | tf_op jit(solution)/shard_map/ppermute | solution.py:27
  12.3 15.4 %collective-permute-start.5 = (bf16[1,2,128,768]{2,3,1,0:T(8,128)(2,1)S(1)}, bf16[1,2,128,768]{2,3,1,0:T(8,128)(2,1)S(1)}, u32[]{:S(2)}, u32[]{:S(2)}) collective-permute-start(bf16[1,2,128,768]{2,3,1,0:T(8,128)(2,1)S(1)} %get-tuple-element.162), channel_id=1, source_target_pairs={{8,0},{16,8},{24,16},{32,24},{40,32},{48,40},{56,48},{64,56},{72,6... | collective-permute-start | bytes 1179656 | tf_op jit(solution)/shard_map/ppermute | solution.py:29
  24.8 29.0 %collective-permute-start.2 = (bf16[6,1,128,768]{2,3,1,0:T(8,128)(2,1)}, bf16[6,1,128,768]{2,3,1,0:T(8,128)(2,1)}, u32[]{:S(2)}, u32[]{:S(2)}) collective-permute-start(bf16[6,1,128,768]{2,3,1,0:T(8,128)(2,1)} %get-tuple-element.159), channel_id=1, source_target_pairs={{0,1},{1,2},{2,3},{3,4},{4,5},{5,6},{6,7},{7,0},{8,9},{9,10},{10,1... | collective-permute-start | bytes 3538952 | tf_op jit(solution)/shard_map/ppermute | solution.py:27
  26.1 53.4 %collective-permute-start.3 = (bf16[6,1,128,768]{2,3,1,0:T(8,128)(2,1)}, bf16[6,1,128,768]{2,3,1,0:T(8,128)(2,1)}, u32[]{:S(2)}, u32[]{:S(2)}) collective-permute-start(bf16[6,1,128,768]{2,3,1,0:T(8,128)(2,1)} %get-tuple-element.160), channel_id=1, source_target_pairs={{1,0},{2,1},{3,2},{4,3},{5,4},{6,5},{7,6},{0,7},{9,8},{10,9},{11,1... | collective-permute-start | bytes 3538952 | tf_op jit(solution)/shard_map/ppermute | solution.py:29
  27.6 1.9 copy-start.3
  27.9 4.2 copy-start.5
  29.6 74.7 %collective-permute-start.6 = (bf16[6,1,128,768]{2,3,1,0:T(8,128)(2,1)}, bf16[6,1,128,768]{2,3,1,0:T(8,128)(2,1)}, u32[]{:S(2)}, u32[]{:S(2)}) collective-permute-start(bf16[6,1,128,768]{2,3,1,0:T(8,128)(2,1)} %get-tuple-element.157), channel_id=1, source_target_pairs={{0,1},{1,2},{2,3},{3,4},{4,5},{5,6},{6,7},{7,0},{8,9},{9,10},{10,1... | collective-permute-start | bytes 3538952 | tf_op jit(solution)/shard_map/ppermute | solution.py:27
  32.1 94.5 %collective-permute-start.7 = (bf16[6,1,128,768]{2,3,1,0:T(8,128)(2,1)}, bf16[6,1,128,768]{2,3,1,0:T(8,128)(2,1)}, u32[]{:S(2)}, u32[]{:S(2)}) collective-permute-start(bf16[6,1,128,768]{2,3,1,0:T(8,128)(2,1)} %get-tuple-element.158), channel_id=1, source_target_pairs={{1,0},{2,1},{3,2},{4,3},{5,4},{6,5},{7,6},{0,7},{9,8},{10,9},{11,1... | collective-permute-start | bytes 3538952 | tf_op jit(solution)/shard_map/ppermute | solution.py:29
  36.2 5.2 copy-start.6
  84.3 42.3 %copy-start.4 = (bf16[1,2,128,768]{2,3,1,0:T(8,128)(2,1)S(1)}, bf16[1,2,128,768]{2,3,1,0:T(8,128)(2,1)}, u32[]{:S(2)}) copy-start(bf16[1,2,128,768]{2,3,1,0:T(8,128)(2,1)} %copy-done.3) | copy-start | bytes 1179652
  174.2 2.3 copy-start.2
  190.6 8.2 copy-start
  226.3 2.3 copy-start.2
  242.7 8.3 copy-start
  278.4 2.3 copy-start.2
  294.8 8.2 copy-start
  330.4 2.3 copy-start.2
  346.8 8.2 copy-start
  382.6 2.3 copy-start.2
  399.0 8.3 copy-start
  434.8 2.3 copy-start.2
  451.2 8.2 copy-start
  486.9 2.3 copy-start.2
  503.3 8.2 copy-start
  539.0 2.3 copy-start.2
  555.4 8.3 copy-start
  570.6 16.1 %copy-start.1 = (f32[24,2,128,12,64]{2,4,3,1,0:T(8,128)S(1)}, f32[24,2,128,12,64]{2,4,3,1,0:T(8,128)}, u32[]{:S(2)}) copy-start(f32[24,2,128,12,64]{2,4,3,1,0:T(8,128)} %get-tuple-element.110) | copy-start | bytes 56623108
  580.1 107.0 %collective-permute-start.8 = (f32[6,1,2,128,768]{3,4,2,1,0:T(8,128)}, f32[6,1,2,128,768]{3,4,2,1,0:T(8,128)}, u32[]{:S(2)}, u32[]{:S(2)}) collective-permute-start(f32[6,1,2,128,768]{3,4,2,1,0:T(8,128)} %get-tuple-element.152), channel_id=1, source_target_pairs={{0,1},{1,2},{2,3},{3,4},{4,5},{5,6},{6,7},{8,9},{9,10},{10,11},{11... | collective-permute-start | bytes 14155784 | tf_op jit(solution)/shard_map/ppermute | solution.py:12
  584.4 203.3 %collective-permute-start.9 = (f32[6,1,2,128,768]{3,4,2,1,0:T(8,128)}, f32[6,1,2,128,768]{3,4,2,1,0:T(8,128)}, u32[]{:S(2)}, u32[]{:S(2)}) collective-permute-start(f32[6,1,2,128,768]{3,4,2,1,0:T(8,128)} %get-tuple-element.151), channel_id=1, source_target_pairs={{1,0},{2,1},{3,2},{4,3},{5,4},{6,5},{7,6},{9,8},{10,9},{11,10},{12... | collective-permute-start | bytes 14155784 | tf_op jit(solution)/shard_map/ppermute | solution.py:12
  795.7 25.9 %collective-permute-start.10 = (bf16[1,2,2,128,768]{3,4,2,1,0:T(8,128)(2,1)S(1)}, bf16[1,2,2,128,768]{3,4,2,1,0:T(8,128)(2,1)S(1)}, u32[]{:S(2)}, u32[]{:S(2)}) collective-permute-start(bf16[1,2,2,128,768]{3,4,2,1,0:T(8,128)(2,1)S(1)} %slice.252), channel_id=1, source_target_pairs={{0,8},{8,16},{16,24},{24,32},{32,40},{40,48},{48,56},{56,64},{64,7... | collective-permute-start | bytes 2359304 | tf_op jit(solution)/shard_map/ppermute | solution.py:17
  824.8 22.1 %collective-permute-start.11 = (f32[1,2,2,128,768]{3,4,2,1,0:T(8,128)S(1)}, f32[1,2,2,128,768]{3,4,2,1,0:T(8,128)S(1)}, u32[]{:S(2)}, u32[]{:S(2)}) collective-permute-start(f32[1,2,2,128,768]{3,4,2,1,0:T(8,128)S(1)} %get-tuple-element.153), channel_id=1, source_target_pairs={{0,120},{8,0},{16,8},{24,16},{32,24},{40,32},{48,40},{56,48},{64,5... | collective-permute-start | bytes 4718600 | tf_op jit(solution)/shard_map/ppermute | solution.py:17
where the time goes:
time: 860 us; the launch traced here: 856 us
  waiting for transfers between devices  304 us (35%)
  local copies, waits for them, and re-layouts  279 us (32%)
  other arithmetic  157 us (18%)
  matrix products  97.3 us (11%)
  starting transfers between devices  18.5 us (2%)
    ppermute x2, waiting for transfers between devices, from_behind(): return lax.ppermute(x, axis, pairs)  191 us
    gather x16, local copies, waits for them, and re-layouts, per_query(): key_sel = key_flat[slot_row]  96.4 us
    scatter-add x8, other arithmetic, per_query(): running = running.at[slot_row, 0].add(key_part)  66 us
    gather x8, local copies, waits for them, and re-layouts, per_query(): value_sel = value_flat[slot_row]  62.1 us
    scatter-add x8, other arithmetic, per_query(): running = running.at[slot_row, 1].add(value_part)  55.3 us
    ppermute x4, waiting for transfers between devices, extended(): lax.ppermute(head, axis, [((i + 1) % count, i) for i in range(count)])  54.1 us
    ppermute x2, waiting for transfers between devices, from_behind_2(): return lax.ppermute(x, axis, [(i, (i + by) % size) for i in range(size)])  39.2 us
    dot_general x8, matrix products, per_query(): jnp.einsum('thd,muhd->htmu', grad_blk, value_sel, preferred_element_type=...  33.3 us
  transfers between devices with their start and end apart: 12, of which 11 were waited for; matrix products, arithmetic and copies ran while one was open for 7% of the time, Pallas kernels for 0%

commit v1 on v0

v1 whole, which is shorter than its diff:
```python
import functools

import jax
import jax.numpy as jnp
from jax import lax
from jax.experimental import pallas as pl
from jax.experimental.pallas import tpu as pltpu
from jax.sharding import PartitionSpec as P

CHUNKS = ((0, 2), (2, 2), (4, 2))
BLK = 128
PAIR = 128
HALF = 64
PAY = 2 * BLK + 16
FAR = 1.0e4
SCALE = 0.125
AXES = ("slit", "span")
VMEM = 56 * 1024 * 1024

NT = (((1,), (1,)), ((), ()))
NN = (((1,), (0,)), ((), ()))


def dot(a, b, dims):
    return lax.dot_general(a, b, dims, preferred_element_type=jnp.float32)


def head_masks():
    lane = lax.broadcasted_iota(jnp.int32, (1, PAIR), 1)
    first = jnp.where(lane < HALF, 1.0, 0.0)
    return first.astype(jnp.bfloat16), (1.0 - first).astype(jnp.bfloat16)


def split_heads(x, masks):
    return jnp.concatenate([x * masks[0], x * masks[1]], axis=0)


def offset_row(dr, dc):
    o = (dr + 1) * 3 + dc + 1
    return 8 if o == 4 else (o if o < 4 else o - 1)


def attend(keys, values, keys_t, queries, masks):
    probs_all, grads_all, q_all, do_all, dq_t = [], [], [], [], []
    for q, do, lse, delta, biases in queries:
        q2 = split_heads(q * jnp.asarray(SCALE, jnp.bfloat16), masks)
        do2 = split_heads(do, masks)
        s = dot(keys, q2, NT)
        dp = dot(values, do2, NT)
        p_parts, g_parts = [], []
        for n, bias in enumerate(biases):
            part = slice(n * BLK, (n + 1) * BLK)
            p = jnp.exp(s[part] - (lse + bias))
            p_parts.append(p.astype(jnp.bfloat16))
            g_parts.append((p * (dp[part] - delta)).astype(jnp.bfloat16))
        p = jnp.concatenate(p_parts, axis=0) if len(p_parts) > 1 else p_parts[0]
        g = jnp.concatenate(g_parts, axis=0) if len(g_parts) > 1 else g_parts[0]
        dq_t.append(
            (dot(keys_t[:HALF], g[:, :BLK], NN), dot(keys_t[HALF:], g[:, BLK:], NN))
        )
        probs_all.append(p)
        grads_all.append(g)
        q_all.append(q2)
        do_all.append(do2)
    cat = lambda xs, axis: jnp.concatenate(xs, axis=axis) if len(xs) > 1 else xs[0]
    dv = dot(cat(probs_all, 1), cat(do_all, 0), NN)
    dk = dot(cat(grads_all, 1), cat(q_all, 0), NN)
    return dk, dv, dq_t


def transpose_keys(k_ref, kt_ref):
    for r in range(4):
        for c in range(2):
            kt_ref[r, :, c * BLK : (c + 1) * BLK] = (
                k_ref[r, c].astype(jnp.float32).T.astype(jnp.bfloat16)
            )


def add_t(ref, index, parts):
    ref[index + (slice(0, HALF),)] += parts[0]
    ref[index + (slice(HALF, PAIR),)] += parts[1]


def prep_kernel(par_ref, q_ref, do_ref, o_ref, lse_ref, used_ref, col0_ref, col1_ref, out_ref, in_ref, dg0_ref, dg1_ref, delta_ref, aux_ref):
    outer = 3 * par_ref[0]
    inner = 3 - outer
    prod = do_ref[...].astype(jnp.float32) * o_ref[...].astype(jnp.float32)
    prod = prod.reshape(8 * BLK, PAIR)
    high = prod.astype(jnp.bfloat16)
    low = (prod - high.astype(jnp.float32)).astype(jnp.bfloat16)
    row = lax.broadcasted_iota(jnp.int32, (16, PAIR), 0)
    lane = lax.broadcasted_iota(jnp.int32, (16, PAIR), 1)
    pick = jnp.where(row == lane // HALF, 1.0, 0.0).astype(jnp.bfloat16)
    delta = dot(pick, high, NT) + dot(pick, low, NT)
    for r in range(4):
        for c in range(2):
            b = 2 * r + c
            d = delta[0:2, b * BLK : (b + 1) * BLK]
            delta_ref[r, c, 0] = d
            for at, x in ((0, lse_ref[r, c, 0]), (4, d)):
                x_high = x.astype(jnp.bfloat16).astype(jnp.float32)
                aux_ref[r, c, at : at + 2] = x_high
                aux_ref[r, c, at + 2 : at + 4] = x - x_high
            aux_ref[r, c, 8:16] = used_ref[r, c, 0:8]

    def pack(dst, at, r, c):
        dst[at, 0:BLK] = q_ref[r, c]
        dst[at, BLK : 2 * BLK] = do_ref[r, c]
        dst[at, 2 * BLK : PAY] = aux_ref[r, c].astype(jnp.bfloat16)

    for r in range(4):
        pack(col0_ref, r, r, 0)
        pack(col1_ref, r, r, 1)
    for c in range(2):
        pack(out_ref, c, outer, c)
        pack(in_ref, c, inner, c)
    pack(dg0_ref, 0, outer, 0)
    pack(dg1_ref, 0, outer, 1)


def local_kernel(q_ref, do_ref, k_ref, v_ref, lse_ref, delta_ref, used_ref, dk_ref, dv_ref, dq_ref, kt_ref, acc_ref):
    masks = head_masks()
    transpose_keys(k_ref, kt_ref)
    acc_ref[...] = jnp.zeros_like(acc_ref)
    dk_ref[...] = jnp.zeros_like(dk_ref)
    dv_ref[...] = jnp.zeros_like(dv_ref)

    def step(n, carry):
        r = (n + 1) // 3
        shift = (n + 1) % 3
        rq = r - 1 + shift
        keys = k_ref[r].reshape(2 * BLK, PAIR)
        values = v_ref[r].reshape(2 * BLK, PAIR)
        queries = []
        for c in range(2):
            lse = lse_ref[rq, c, 0]
            delta = delta_ref[rq, c, 0]
            biases = []
            for kc in range(2):
                o = (2 - shift) * 3 + kc - c + 1
                o = jnp.where(o == 4, 8, jnp.where(o > 4, o - 1, o))
                used = used_ref[rq, c, pl.ds(o, 1), :]
                bias = (1.0 - used) * FAR
                biases.append(jnp.concatenate([bias, bias], axis=1))
            queries.append(
                (
                    q_ref[rq, c],
                    do_ref[rq, c],
                    jnp.concatenate([lse[0:1], lse[1:2]], axis=1),
                    jnp.concatenate([delta[0:1], delta[1:2]], axis=1),
                    biases,
                )
            )
        dk, dv, dq_t = attend(keys, values, kt_ref[r], queries, masks)
        dk_ref[r] += dk.reshape(2, BLK, PAIR)
        dv_ref[r] += dv.reshape(2, BLK, PAIR)
        for c in range(2):
            add_t(acc_ref, (rq, c), dq_t[c])
        return carry

    lax.fori_loop(0, 10, step, 0)
    for r in range(4):
        for c in range(2):
            dq_ref[r, c] = acc_ref[r, c].T * SCALE


def remote_kernel(par_ref, k_ref, v_ref, col0_ref, col1_ref, out_ref, in_ref, dg0_ref, dg1_ref, dkp_ref, dvp_ref, *rest):
    dk_ref, dv_ref, r0_ref, r1_ref, ro_ref, ri_ref, rg0_ref, rg1_ref, kt_ref, acck_ref, accv_ref, accq_ref, aux_ref = rest[-13:]
    masks = head_masks()
    par = par_ref[0]
    outer = 3 * par
    inner = 3 - outer
    transpose_keys(k_ref, kt_ref)
    acck_ref[...] = dkp_ref[...]
    accv_ref[...] = dvp_ref[...]
    slots = (
        [(col0_ref, i) for i in range(4)]
        + [(col1_ref, i) for i in range(4)]
        + [(out_ref, 0), (out_ref, 1)]
        + [(in_ref, i) for i in range(4)]
        + [(dg0_ref, 0), (dg1_ref, 0)]
    )
    for i, (ref, at) in enumerate(slots):
        aux_ref[i] = ref[at, 2 * BLK : PAY].astype(jnp.float32)

    def query(i, rows):
        ref, at = slots[i]
        stats = aux_ref[i, 0:8]
        lse = stats[0:2] + stats[2:4]
        delta = stats[4:6] + stats[6:8]
        biases = []
        for row in rows:
            bias = (1.0 - aux_ref[i, pl.ds(8 + row, 1), :]) * FAR
            biases.append(jnp.concatenate([bias, bias], axis=1))
        return (
            ref[at, 0:BLK],
            ref[at, BLK : 2 * BLK],
            jnp.concatenate([lse[0:1], lse[1:2]], axis=1),
            jnp.concatenate([delta[0:1], delta[1:2]], axis=1),
            biases,
        )

    def put(i, parts):
        accq_ref[i, 0:HALF] = parts[0]
        accq_ref[i, HALF:PAIR] = parts[1]

    for side in range(2):
        dc = 1 - 2 * side
        lanes = slice(side * BLK, (side + 1) * BLK)
        for a in (0, 2):
            keys = jnp.concatenate([k_ref[a, side], k_ref[a + 1, side]], axis=0)
            values = jnp.concatenate([v_ref[a, side], v_ref[a + 1, side]], axis=0)
            keys_t = jnp.concatenate([kt_ref[a, :, lanes], kt_ref[a + 1, :, lanes]], axis=1)
            queries = [
                query(4 * side + a, [offset_row(0, dc), offset_row(1, dc)]),
                query(4 * side + a + 1, [offset_row(-1, dc), offset_row(0, dc)]),
            ]
            dk, dv, dq_t = attend(keys, values, keys_t, queries, masks)
            for n in range(2):
                part = slice(n * BLK, (n + 1) * BLK)
                acck_ref[a + n, side] += dk[part]
                accv_ref[a + n, side] += dv[part]
                put(4 * side + a + n, dq_t[n])
    up, down = 0, 5
    row_outer = jnp.where(par == 0, down, up)
    row_inner = down + up - row_outer
    for side in range(2):
        dc = 1 - 2 * side
        lanes = slice(side * BLK, (side + 1) * BLK)
        singles = [
            (1, 4 * side + 2, offset_row(-1, dc), True),
            (2, 4 * side + 1, offset_row(1, dc), True),
            (outer, 14 + side, row_outer + dc + 1, False),
            (inner, 12 + side, row_inner + dc + 1, False),
        ]
        for r, i, row, more in singles:
            dk, dv, dq_t = attend(
                k_ref[r, side], v_ref[r, side], kt_ref[r, :, lanes], [query(i, [row])], masks
            )
            acck_ref[r, side] += dk
            accv_ref[r, side] += dv
            if more:
                add_t(accq_ref, (i,), dq_t[0])
            else:
                put(i, dq_t[0])
    for r, first, row in ((outer, 8, row_outer), (inner, 10, row_inner)):
        queries = [query(first + c, [row + kc - c + 1 for kc in range(2)]) for c in range(2)]
        dk, dv, dq_t = attend(
            k_ref[r].reshape(2 * BLK, PAIR), v_ref[r].reshape(2 * BLK, PAIR), kt_ref[r], queries, masks
        )
        acck_ref[r] += dk.reshape(2, BLK, PAIR)
        accv_ref[r] += dv.reshape(2, BLK, PAIR)
        for c in range(2):
            put(first + c, dq_t[c])
    dk_ref[...] = acck_ref[...].astype(jnp.bfloat16)
    dv_ref[...] = accv_ref[...].astype(jnp.bfloat16)
    targets = (
        [(r0_ref, i) for i in range(4)]
        + [(r1_ref, i) for i in range(4)]
        + [(ro_ref, 0), (ro_ref, 1)]
        + [(ri_ref, i) for i in range(4)]
        + [(rg0_ref, 0), (rg1_ref, 0)]
    )
    for i, (ref, at) in enumerate(targets):
        ref[at] = (accq_ref[i].T * SCALE).astype(jnp.bfloat16)


def finish_kernel(par_ref, dq_ref, b0_ref, b1_ref, bo_ref, bi_ref, bg0_ref, bg1_ref, *rest):
    res_ref, acc_ref = rest[-2:]
    outer = 3 * par_ref[0]
    inner = 3 - outer
    f32 = jnp.float32
    for r in range(4):
        acc_ref[r, 0] = dq_ref[r, 0] + b0_ref[r].astype(f32)
        acc_ref[r, 1] = dq_ref[r, 1] + b1_ref[r].astype(f32)
    for c in range(2):
        acc_ref[outer, c] += bo_ref[c].astype(f32)
        acc_ref[inner, c] += bi_ref[c].astype(f32)
    acc_ref[outer, 0] += bg0_ref[0].astype(f32)
    acc_ref[outer, 1] += bg1_ref[0].astype(f32)
    res_ref[...] = acc_ref[...].astype(jnp.bfloat16)


def spec(shape, base=0):
    zeros = (0,) * (len(shape) - 1)
    return pl.BlockSpec(shape, lambda h: zeros + (h + base,))


def pair_spec(base=0):
    return pl.BlockSpec((4, 2, 1, 2, BLK), lambda h: (0, 0, h + base, 0, 0))


def used_spec():
    return pl.BlockSpec((4, 2, 16, BLK), lambda h: (0, 0, 0, 0))


SMEM = pl.BlockSpec(memory_space=pltpu.SMEM)
ANY = pl.BlockSpec(memory_space=pl.ANY)
TILES = (4, 2, BLK, PAIR)


def params():
    return pltpu.CompilerParams(vmem_limit_bytes=VMEM, dimension_semantics=("arbitrary",))


def cost(pairs, count):
    return pl.CostEstimate(
        flops=pairs * count * 2 * 5 * 2 * BLK * BLK * HALF * 4,
        bytes_accessed=pairs * count * 4 * BLK * PAIR * 2,
        transcendentals=pairs * count * 2 * BLK * BLK,
    )


def sds(shape, dtype=jnp.bfloat16):
    return jax.ShapeDtypeStruct(shape, dtype)


def prep(par, q, do, o, lse, used, base, count):
    width = count * PAIR
    shapes = [4, 4, 2, 2, 1, 1]
    return pl.pallas_call(
        prep_kernel,
        grid=(count,),
        in_specs=[SMEM] + [spec(TILES, base)] * 3 + [pair_spec(base), used_spec()],
        out_specs=[spec((n, PAY, PAIR)) for n in shapes] + [pair_spec()],
        out_shape=[sds((n, PAY, width)) for n in shapes] + [sds((4, 2, count, 2, BLK), jnp.float32)],
        scratch_shapes=[pltpu.VMEM((4, 2, 16, BLK), jnp.float32)],
        compiler_params=params(),
        name="prep",
    )(par, q, do, o, lse, used)


def local(q, do, k, v, lse, delta, used, base, count):
    width = count * PAIR
    full = sds((4, 2, BLK, width), jnp.float32)
    return pl.pallas_call(
        local_kernel,
        grid=(count,),
        in_specs=[spec(TILES, base)] * 4 + [pair_spec(base), pair_spec(), used_spec()],
        out_specs=[spec(TILES)] * 3,
        out_shape=[full] * 3,
        scratch_shapes=[
            pltpu.VMEM((4, PAIR, 2 * BLK), jnp.bfloat16),
            pltpu.VMEM(TILES, jnp.float32),
        ],
        compiler_params=params(),
        cost_estimate=cost(40, count),
        name="local",
    )(q, do, k, v, lse, delta, used)


def remote(par, k, v, halo, dkp, dvp, done, base, count):
    width = count * PAIR
    sizes = [4, 4, 2, 4, 1, 1]
    full = sds((4, 2, BLK, 6 * PAIR))
    return pl.pallas_call(
        remote_kernel,
        grid=(count,),
        in_specs=[SMEM]
        + [spec(TILES, base)] * 2
        + [spec((n, PAY, PAIR)) for n in sizes]
        + [spec(TILES)] * 2
        + [ANY] * len(done),
        out_specs=[spec(TILES, base)] * 2 + [spec((n, BLK, PAIR)) for n in sizes],
        out_shape=[full] * 2 + [sds((n, BLK, width)) for n in sizes],
        input_output_aliases={11 + i: i for i in range(len(done))},
        scratch_shapes=[
            pltpu.VMEM((4, PAIR, 2 * BLK), jnp.bfloat16),
            pltpu.VMEM(TILES, jnp.float32),
            pltpu.VMEM(TILES, jnp.float32),
            pltpu.VMEM((16, PAIR, BLK), jnp.float32),
            pltpu.VMEM((16, 16, BLK), jnp.float32),
        ],
        compiler_params=params(),
        cost_estimate=cost(32, count),
        name="remote",
    )(par, k, v, *halo, dkp, dvp, *done)


def finish(par, dqp, back, done, base, count):
    sizes = [4, 4, 2, 2, 1, 1]
    return pl.pallas_call(
        finish_kernel,
        grid=(count,),
        in_specs=[SMEM, spec(TILES)] + [spec((n, BLK, PAIR)) for n in sizes] + [ANY] * len(done),
        out_specs=spec(TILES, base),
        out_shape=sds((4, 2, BLK, 6 * PAIR)),
        input_output_aliases={8 + i: i for i in range(len(done))},
        scratch_shapes=[pltpu.VMEM(TILES, jnp.float32)],
        compiler_params=params(),
        name="finish",
    )(par, dqp, *back, *done)


def pairs_of(rows, cols):
    at = lambda s, p: (s % rows) * cols + p
    outer = lambda s: s + 1 if s % 2 else s - 1
    inner = lambda s: s - 1 if s % 2 else s + 1
    cells = [(s, p) for s in range(rows) for p in range(cols)]
    return {
        "right": [(at(s, p), at(s, p + 1)) for s, p in cells if p + 1 < cols],
        "left": [(at(s, p), at(s, p - 1)) for s, p in cells if p > 0],
        "outer": [(at(s, p), at(outer(s), p)) for s, p in cells],
        "inner": [(at(s, p), at(inner(s), p)) for s, p in cells],
        "outer_right": [(at(s, p), at(outer(s), p + 1)) for s, p in cells if p + 1 < cols],
        "outer_left": [(at(s, p), at(outer(s), p - 1)) for s, p in cells if p > 0],
    }


def list_masks(neighbours, flags, grid_a, grid_b):
    rows_a, rows_b = neighbours.shape[:2]
    a = lax.axis_index("slit") * rows_a + lax.broadcasted_iota(jnp.int32, (rows_a, rows_b, 16), 0)
    b = lax.axis_index("span") * rows_b + lax.broadcasted_iota(jnp.int32, (rows_a, rows_b, 16), 1)
    row = lax.broadcasted_iota(jnp.int32, (rows_a, rows_b, 16), 2)
    o = jnp.where(row == 8, 4, jnp.where(row < 4, row, row + 1))
    to_a = (a + o // 3 - 1 + grid_a) % grid_a
    to_b = b + o % 3 - 1
    valid = (row < 9) & (to_b >= 0) & (to_b < grid_b)
    ids = jnp.where(valid, to_a * grid_b + to_b, -1)
    hit = (neighbours[:, :, None, :] == ids[:, :, :, None]) & (flags[:, :, None, :] != 0)
    used = jnp.any(hit, axis=-1).astype(jnp.float32)
    return jnp.broadcast_to(used[:, :, :, None], (rows_a, rows_b, 16, BLK))


def on_device(rows, cols, q, k, v, o, do, lse, neighbours, flags):
    pairs = pairs_of(rows, cols)
    send = lambda x, way: lax.ppermute(x, AXES, pairs[way])
    par = lax.axis_index("slit") % 2
    pars = par.reshape(1).astype(jnp.int32)
    inner_row = 3 - 3 * par
    used = list_masks(neighbours, flags, 4 * rows, 2 * cols)
    lse = lse.reshape(4, 2, 6, 2, BLK)

    dks, dqs = (), ()
    for base, count in CHUNKS:
        col0, col1, out, inn, dg0, dg1, delta = prep(pars, q, do, o, lse, used, base, count)
        from_left = send(col1, "right")
        from_right = send(col0, "left")
        halo_out = send(out, "outer")
        halo_g0 = send(dg1, "outer_right")
        halo_g1 = send(dg0, "outer_left")
        dkp, dvp, dqp = local(q, do, k, v, lse, delta, used, base, count)
        corner0 = lax.dynamic_slice_in_dim(from_left, inner_row, 1, 0)
        corner1 = lax.dynamic_slice_in_dim(from_right, inner_row, 1, 0)
        halo_in = send(jnp.concatenate([inn, corner0, corner1], axis=0), "inner")
        halo = (from_left, from_right, halo_out, halo_in, halo_g0, halo_g1)
        dk, dv, r0, r1, ro, ri, rg0, rg1 = remote(pars, k, v, halo, dkp, dvp, dks, base, count)
        dks = (dk, dv)
        back_in = send(ri, "inner")
        index = (inner_row, 0, 0)
        r0 = lax.dynamic_update_slice(
            r0, lax.dynamic_slice_in_dim(r0, inner_row, 1, 0) + back_in[2:3], index
        )
        r1 = lax.dynamic_update_slice(
            r1, lax.dynamic_slice_in_dim(r1, inner_row, 1, 0) + back_in[3:4], index
        )
        back1 = send(r0, "left")
        back0 = send(r1, "right")
        back_out = send(ro, "outer")
        back_g1 = send(rg0, "outer_left")
        back_g0 = send(rg1, "outer_right")
        back = (back0, back1, back_out, back_in[0:2], back_g0, back_g1)
        dqs = (finish(pars, dqp, back, dqs, base, count),)
    return dqs[0], dks[0], dks[1]


def solution(mesh):
    tile = P("slit", "span", None, None)
    row = P("slit", "span", None)
    body = functools.partial(on_device, mesh.shape["slit"], mesh.shape["span"])
    return jax.shard_map(
        body,
        mesh=mesh,
        in_specs=(tile,) * 6 + (row,) * 2,
        out_specs=(tile,) * 3,
        check_vma=False,
    )
```

time: 860 us -> 260 us (0.30)
  the two profiles are of different devices: /device:TPU:71 before, /device:TPU:96 now
where the time goes in v1:
time: 260 us; the launch traced here: 259 us
  Pallas kernels  116 us (45%)
  starting transfers between devices  115 us (44%)
  waiting for transfers between devices  15 us (6%)
  local copies, waits for them, and re-layouts  7.34 us (3%)
  other arithmetic  3.43 us (1%)
    ppermute x36, starting transfers between devices, on_device(): send = lambda x, way: lax.ppermute(x, AXES, pairs[way])  115 us
    pallas_call x3, Pallas kernels, local(): pl.pallas_call(local_kernel, grid=(count,), in_specs=[spec(TILES, base)]...  57.1 us
    pallas_call x3, Pallas kernels, remote(): pl.pallas_call(remote_kernel, grid=(count,), in_specs=[SMEM] + [spec(TILE...  43.1 us
    ppermute x36, waiting for transfers between devices, on_device(): send = lambda x, way: lax.ppermute(x, AXES, pairs[way])  15 us
    pallas_call x3, Pallas kernels, prep(): pl.pallas_call(prep_kernel, grid=(count,), in_specs=[SMEM] + [spec(TILES,...  8.81 us
    pallas_call x3, Pallas kernels, finish(): pl.pallas_call(finish_kernel, grid=(count,), in_specs=[SMEM, spec(TILES)]...  7 us
  transfers between devices with their start and end apart: 36, of which 2 were waited for; matrix products, arithmetic and copies ran while one was open for 2% of the time, Pallas kernels for 43%

profile of v1, /device:TPU:96, one launch (start us, length us, event | category | flops | bytes accessed | tf_op | source)
XLA Modules:
  0.0 258.6 jit_solution(10176953909749452634)
XLA Ops:
  0.7 0.7 broadcast_compare_fusion
  1.4 0.1 and_select_fusion.2
  1.5 0.8 and_reduce_fusion
  2.3 1.4 copy.25.lse_ref
  3.7 0.7 broadcast_in_dim.19.used_ref
  4.4 3.0 %prep.5 = (bf16[4,272,256]{2,1,0:T(8,128)(2,1)}, bf16[4,272,256]{2,1,0:T(8,128)(2,1)}, bf16[2,272,256]{2,1,0:T(8,128)(2,1)}, bf16[2,272,256]{2,1,0:T(8,128)(2,1)...) custom-call(s32[1]{0:T(128)} %bitcast.par_ref, ...), custom_call_target="tpu_custom_call" | custom-call | tf_op jit(solution)/shard_map/prep/pallas_call | solution.py:321
  7.4 3.3 %collective-permute-start.13 = (bf16[4,272,256]{2,1,0:T(8,128)(2,1)}, bf16[4,272,256]{2,1,0:T(8,128)(2,1)S(1)}, u32[]{:S(2)}, u32[]{:S(2)}) collective-permute-start(bf16[4,272,256]{2,1,0:T(8,128)(2,1)} %get-tuple-element.77), channel_id=1, source_target_pairs={{1,0},{2,1},{3,2},{4,3},{5,4},{6,5},{7,6},{9,8},{10,9},{11,10},{12... | collective-permute-start | bytes 1671176 | tf_op jit(solution)/shard_map/ppermute | solution.py:427
  10.7 2.5 collective-permute-start.12
  13.3 4.3 %collective-permute-start.14 = (bf16[2,272,256]{2,1,0:T(8,128)(2,1)}, bf16[2,272,256]{2,1,0:T(8,128)(2,1)}, u32[]{:S(2)}, u32[]{:S(2)}) collective-permute-start(bf16[2,272,256]{2,1,0:T(8,128)(2,1)} %get-tuple-element.78), channel_id=1, source_target_pairs={{0,120},{1,121},{2,122},{3,123},{4,124},{5,125},{6,126},{7,127},{8... | collective-permute-start | bytes 835592 | tf_op jit(solution)/shard_map/ppermute | solution.py:427
  17.6 2.9 %prep.4 = (bf16[4,272,256]{2,1,0:T(8,128)(2,1)}, bf16[4,272,256]{2,1,0:T(8,128)(2,1)}, bf16[2,272,256]{2,1,0:T(8,128)(2,1)}, bf16[2,272,256]{2,1,0:T(8,128)(2,1)...) custom-call(s32[1]{0:T(128)} %bitcast.par_ref, ...), custom_call_target="tpu_custom_call" | custom-call | tf_op jit(solution)/shard_map/prep/pallas_call | solution.py:321
  20.6 3.3 %collective-permute-start.7 = (bf16[4,272,256]{2,1,0:T(8,128)(2,1)}, bf16[4,272,256]{2,1,0:T(8,128)(2,1)S(1)}, u32[]{:S(2)}, u32[]{:S(2)}) collective-permute-start(bf16[4,272,256]{2,1,0:T(8,128)(2,1)} %get-tuple-element.68), channel_id=1, source_target_pairs={{1,0},{2,1},{3,2},{4,3},{5,4},{6,5},{7,6},{9,8},{10,9},{11,10},{12... | collective-permute-start | bytes 1671176 | tf_op jit(solution)/shard_map/ppermute | solution.py:427
  23.9 2.6 collective-permute-start.6
  26.4 2.9 %prep.3 = (bf16[4,272,256]{2,1,0:T(8,128)(2,1)}, bf16[4,272,256]{2,1,0:T(8,128)(2,1)}, bf16[2,272,256]{2,1,0:T(8,128)(2,1)}, bf16[2,272,256]{2,1,0:T(8,128)(2,1)...) custom-call(s32[1]{0:T(128)} %bitcast.par_ref, ...), custom_call_target="tpu_custom_call" | custom-call | tf_op jit(solution)/shard_map/prep/pallas_call | solution.py:321
  29.4 19.0 %local.5 = (f32[4,2,128,256]{3,2,1,0:T(8,128)}, f32[4,2,128,256]{3,2,1,0:T(8,128)}, f32[4,2,128,256]{3,2,1,0:T(8,128)}) custom-call(bf16[4,2,128,768]{3,2,1,0:T(8,128)(2,1)} %q_ref.11, bf16[4,2,128,768]{3,2,1,0:T(8,128)(2,1)} %do_ref.11, bf16[4,2,128,768]{3,2,1,0:T(8,128)(2,1)} %k_ref.11, bf16[4,2,128,768]{3,2,1,0:T(8,128)(2,1)} %v_ref.11, ...), custom_call_target="tpu_custom_call" | custom-call | flops 6710886400 | bytes 10485760 | tf_op jit(solution)/shard_map/local/pallas_call | solution.py:336
  48.4 19.0 %local.4 = (f32[4,2,128,256]{3,2,1,0:T(8,128)}, f32[4,2,128,256]{3,2,1,0:T(8,128)}, f32[4,2,128,256]{3,2,1,0:T(8,128)}) custom-call(bf16[4,2,128,768]{3,2,1,0:T(8,128)(2,1)} %q_ref.11, bf16[4,2,128,768]{3,2,1,0:T(8,128)(2,1)} %do_ref.11, bf16[4,2,128,768]{3,2,1,0:T(8,128)(2,1)} %k_ref.11, bf16[4,2,128,768]{3,2,1,0:T(8,128)(2,1)} %v_ref.11, ...), custom_call_target="tpu_custom_call" | custom-call | flops 6710886400 | bytes 10485760 | tf_op jit(solution)/shard_map/local/pallas_call | solution.py:336
  67.4 19.1 %local.3 = (f32[4,2,128,256]{3,2,1,0:T(8,128)}, f32[4,2,128,256]{3,2,1,0:T(8,128)}, f32[4,2,128,256]{3,2,1,0:T(8,128)}) custom-call(bf16[4,2,128,768]{3,2,1,0:T(8,128)(2,1)} %q_ref.11, bf16[4,2,128,768]{3,2,1,0:T(8,128)(2,1)} %do_ref.11, bf16[4,2,128,768]{3,2,1,0:T(8,128)(2,1)} %k_ref.11, bf16[4,2,128,768]{3,2,1,0:T(8,128)(2,1)} %v_ref.11, ...), custom_call_target="tpu_custom_call" | custom-call | flops 6710886400 | bytes 10485760 | tf_op jit(solution)/shard_map/local/pallas_call | solution.py:336
  86.5 2.1 collective-permute-start.16
  88.6 4.5 %collective-permute-start.1 = (bf16[4,272,256]{2,1,0:T(8,128)(2,1)}, bf16[4,272,256]{2,1,0:T(8,128)(2,1)S(1)}, u32[]{:S(2)}, u32[]{:S(2)}) collective-permute-start(bf16[4,272,256]{2,1,0:T(8,128)(2,1)} %get-tuple-element.60), channel_id=1, source_target_pairs={{1,0},{2,1},{3,2},{4,3},{5,4},{6,5},{7,6},{9,8},{10,9},{11,10},{12... | collective-permute-start | bytes 1671176 | tf_op jit(solution)/shard_map/ppermute | solution.py:427
  93.2 1.9 collective-permute-start
  95.3 0.1 collective-permute-start.15
  95.6 11.0 %collective-permute-done.1.col1_ref = bf16[4,272,256]{2,1,0:T(8,128)(2,1)S(1)} collective-permute-done((bf16[4,272,256]{2,1,0:T(8,128)(2,1)}, bf16[4,272,256]{2,1,0:T(8,128)(2,1)S(1)}, u32[]{:S(2)}, u32[]{:S(2)}) %collective-permute-start.1) | collective-permute-done | bytes 557088 | tf_op jit(solution)/shard_map/ppermute | solution.py:427
  106.6 7.4 %collective-permute-start.17 = (bf16[1,272,256]{2,1,0:T(8,128)(2,1)S(1)}, bf16[1,272,256]{2,1,0:T(8,128)(2,1)S(1)}, u32[]{:S(2)}, u32[]{:S(2)}) collective-permute-start(bf16[1,272,256]{2,1,0:T(8,128)(2,1)S(1)} %copy-done.40), channel_id=1, source_target_pairs={{1,120},{2,121},{3,122},{4,123},{5,124},{6,125},{7,126},{9,16},{10... | collective-permute-start | bytes 417800 | tf_op jit(solution)/shard_map/ppermute | solution.py:427
  114.0 3.9 %collective-permute-done.col0_ref = bf16[4,272,256]{2,1,0:T(8,128)(2,1)S(1)} collective-permute-done((bf16[4,272,256]{2,1,0:T(8,128)(2,1)S(1)}, bf16[4,272,256]{2,1,0:T(8,128)(2,1)S(1)}, u32[]{:S(2)}, u32[]{:S(2)}) %collective-permute-start) | collective-permute-done | bytes 557088 | tf_op jit(solution)/shard_map/ppermute | solution.py:427
  118.0 4.5 %collective-permute-start.8 = (bf16[2,272,256]{2,1,0:T(8,128)(2,1)S(1)}, bf16[2,272,256]{2,1,0:T(8,128)(2,1)S(1)}, u32[]{:S(2)}, u32[]{:S(2)}) collective-permute-start(bf16[2,272,256]{2,1,0:T(8,128)(2,1)S(1)} %copy-done.33), channel_id=1, source_target_pairs={{0,120},{1,121},{2,122},{3,123},{4,124},{5,125},{6,126},{7,127},{8... | collective-permute-start | bytes 835592 | tf_op jit(solution)/shard_map/ppermute | solution.py:427
  122.6 2.1 collective-permute-start.10
  124.7 7.6 %collective-permute-start.11 = (bf16[1,272,256]{2,1,0:T(8,128)(2,1)S(1)}, bf16[1,272,256]{2,1,0:T(8,128)(2,1)S(1)}, u32[]{:S(2)}, u32[]{:S(2)}) collective-permute-start(bf16[1,272,256]{2,1,0:T(8,128)(2,1)S(1)} %copy-done.38), channel_id=1, source_target_pairs={{1,120},{2,121},{3,122},{4,123},{5,124},{6,125},{7,126},{9,16},{10... | collective-permute-start | bytes 417800 | tf_op jit(solution)/shard_map/ppermute | solution.py:427
  132.4 0.1 collective-permute-start.3
  132.5 0.7 copy-done.31
  133.2 14.3 %remote.3 = (bf16[4,2,128,768]{3,2,1,0:T(8,128)(2,1)}, bf16[4,2,128,768]{3,2,1,0:T(8,128)(2,1)}, bf16[4,128,256]{2,1,0:T(8,128)(2,1)}, bf16[4,128,256]{2,1,0:T(8...) custom-call(s32[1]{0:T(128)} %bitcast.par_ref, ...), custom_call_target="tpu_custom_call" | custom-call | flops 5368709120 | bytes 8388608 | tf_op jit(solution)/shard_map/remote/pallas_call | solution.py:356
  147.6 0.1 collective-permute-start.2
  147.7 4.9 %collective-permute-start.4 = (bf16[1,272,256]{2,1,0:T(8,128)(2,1)S(1)}, bf16[1,272,256]{2,1,0:T(8,128)(2,1)S(1)}, u32[]{:S(2)}, u32[]{:S(2)}) collective-permute-start(bf16[1,272,256]{2,1,0:T(8,128)(2,1)S(1)} %copy-done.37), channel_id=1, source_target_pairs={{0,121},{1,122},{2,123},{3,124},{4,125},{5,126},{6,127},{8,17},{9,... | collective-permute-start | bytes 417800 | tf_op jit(solution)/shard_map/ppermute | solution.py:427
  152.7 4.8 %collective-permute-start.5 = (bf16[1,272,256]{2,1,0:T(8,128)(2,1)S(1)}, bf16[1,272,256]{2,1,0:T(8,128)(2,1)S(1)}, u32[]{:S(2)}, u32[]{:S(2)}) collective-permute-start(bf16[1,272,256]{2,1,0:T(8,128)(2,1)S(1)} %copy-done.36), channel_id=1, source_target_pairs={{1,120},{2,121},{3,122},{4,123},{5,124},{6,125},{7,126},{9,16},{10... | collective-permute-start | bytes 417800 | tf_op jit(solution)/shard_map/ppermute | solution.py:427
  157.6 0.1 collective-permute-start.30
  157.7 0.7 copy-done.29
  158.4 14.3 %remote.4 = (bf16[4,2,128,768]{3,2,1,0:T(8,128)(2,1)}, bf16[4,2,128,768]{3,2,1,0:T(8,128)(2,1)}, bf16[4,128,256]{2,1,0:T(8,128)(2,1)}, bf16[4,128,256]{2,1,0:T(8...) custom-call(s32[1]{0:T(128)} %bitcast.par_ref, ...), custom_call_target="tpu_custom_call", output_to_operand_aliasing={{0}: (11, {}), {1}: (12, {})} | custom-call | flops 5368709120 | bytes 8388608 | tf_op jit(solution)/shard_map/remote/pallas_call | solution.py:356
  172.8 4.2 %collective-permute-start.33 = (bf16[2,128,256]{2,1,0:T(8,128)(2,1)S(1)}, bf16[2,128,256]{2,1,0:T(8,128)(2,1)S(1)}, u32[]{:S(2)}, u32[]{:S(2)}) collective-permute-start(bf16[2,128,256]{2,1,0:T(8,128)(2,1)S(1)} %copy-done.48), channel_id=1, source_target_pairs={{0,120},{1,121},{2,122},{3,123},{4,124},{5,125},{6,126},{7,127},{8... | collective-permute-start | bytes 393224 | tf_op jit(solution)/shard_map/ppermute | solution.py:427
  177.0 1.9 collective-permute-start.34
  178.9 7.9 %collective-permute-start.35 = (bf16[1,128,256]{2,1,0:T(8,128)(2,1)S(1)}, bf16[1,128,256]{2,1,0:T(8,128)(2,1)S(1)}, u32[]{:S(2)}, u32[]{:S(2)}) collective-permute-start(bf16[1,128,256]{2,1,0:T(8,128)(2,1)S(1)} %copy-done.50), channel_id=1, source_target_pairs={{1,120},{2,121},{3,122},{4,123},{5,124},{6,125},{7,126},{9,16},{10... | collective-permute-start | bytes 196616 | tf_op jit(solution)/shard_map/ppermute | solution.py:427
  186.8 0.1 collective-permute-start.24
  186.9 0.7 copy-done.28
  187.7 14.4 %remote.5 = (bf16[4,2,128,768]{3,2,1,0:T(8,128)(2,1)}, bf16[4,2,128,768]{3,2,1,0:T(8,128)(2,1)}, bf16[4,128,256]{2,1,0:T(8,128)(2,1)}, bf16[4,128,256]{2,1,0:T(8...) custom-call(s32[1]{0:T(128)} %bitcast.par_ref, ...), custom_call_target="tpu_custom_call", output_to_operand_aliasing={{0}: (11, {}), {1}: (12, {})} | custom-call | flops 5368709120 | bytes 8388608 | tf_op jit(solution)/shard_map/remote/pallas_call | solution.py:356
  202.1 0.1 collective-permute-start.18
  202.3 1.9 collective-permute-start.28
  204.2 7.9 %collective-permute-start.29 = (bf16[1,128,256]{2,1,0:T(8,128)(2,1)S(1)}, bf16[1,128,256]{2,1,0:T(8,128)(2,1)S(1)}, u32[]{:S(2)}, u32[]{:S(2)}) collective-permute-start(bf16[1,128,256]{2,1,0:T(8,128)(2,1)S(1)} %copy-done.52), channel_id=1, source_target_pairs={{1,120},{2,121},{3,122},{4,123},{5,124},{6,125},{7,126},{9,16},{10... | collective-permute-start | bytes 196616 | tf_op jit(solution)/shard_map/ppermute | solution.py:427
  212.1 1.9 collective-permute-start.31
  214.1 0.4 collective-permute-start.27
  214.5 4.6 %collective-permute-start.32 = (bf16[4,128,256]{2,1,0:T(8,128)(2,1)S(1)}, bf16[4,128,256]{2,1,0:T(8,128)(2,1)S(1)}, u32[]{:S(2)}, u32[]{:S(2)}) collective-permute-start(bf16[4,128,256]{2,1,0:T(8,128)(2,1)S(1)} %get-tuple-element.111), channel_id=1, source_target_pairs={{1,0},{2,1},{3,2},{4,3},{5,4},{6,5},{7,6},{9,8},{10,9},{11,10},{12... | collective-permute-start | bytes 786440 | tf_op jit(solution)/shard_map/ppermute | solution.py:427
  219.1 1.9 collective-permute-start.25
  221.0 4.8 %collective-permute-start.26 = (bf16[4,128,256]{2,1,0:T(8,128)(2,1)S(1)}, bf16[4,128,256]{2,1,0:T(8,128)(2,1)S(1)}, u32[]{:S(2)}, u32[]{:S(2)}) collective-permute-start(bf16[4,128,256]{2,1,0:T(8,128)(2,1)S(1)} %get-tuple-element.113), channel_id=1, source_target_pairs={{1,0},{2,1},{3,2},{4,3},{5,4},{6,5},{7,6},{9,8},{10,9},{11,10},{12... | collective-permute-start | bytes 786440 | tf_op jit(solution)/shard_map/ppermute | solution.py:427
  225.9 1.6 fusion.4
  227.4 1.9 collective-permute-start.19
  229.4 4.8 %collective-permute-start.20 = (bf16[4,128,256]{2,1,0:T(8,128)(2,1)}, bf16[4,128,256]{2,1,0:T(8,128)(2,1)S(1)}, u32[]{:S(2)}, u32[]{:S(2)}) collective-permute-start(bf16[4,128,256]{2,1,0:T(8,128)(2,1)} %get-tuple-element.115), channel_id=1, source_target_pairs={{1,0},{2,1},{3,2},{4,3},{5,4},{6,5},{7,6},{9,8},{10,9},{11,10},{12... | collective-permute-start | bytes 786440 | tf_op jit(solution)/shard_map/ppermute | solution.py:427
  234.2 4.6 %collective-permute-start.21 = (bf16[2,128,256]{2,1,0:T(8,128)(2,1)}, bf16[2,128,256]{2,1,0:T(8,128)(2,1)S(1)}, u32[]{:S(2)}, u32[]{:S(2)}) collective-permute-start(bf16[2,128,256]{2,1,0:T(8,128)(2,1)} %get-tuple-element.92), channel_id=1, source_target_pairs={{0,120},{1,121},{2,122},{3,123},{4,124},{5,125},{6,126},{7,127},{8... | collective-permute-start | bytes 393224 | tf_op jit(solution)/shard_map/ppermute | solution.py:427
  238.8 2.0 collective-permute-start.22
  240.9 7.8 %collective-permute-start.23 = (bf16[1,128,256]{2,1,0:T(8,128)(2,1)}, bf16[1,128,256]{2,1,0:T(8,128)(2,1)S(1)}, u32[]{:S(2)}, u32[]{:S(2)}) collective-permute-start(bf16[1,128,256]{2,1,0:T(8,128)(2,1)} %get-tuple-element.94), channel_id=1, source_target_pairs={{1,120},{2,121},{3,122},{4,123},{5,124},{6,125},{7,126},{9,16},{10... | collective-permute-start | bytes 196616 | tf_op jit(solution)/shard_map/ppermute | solution.py:427
  248.6 0.7 slice.44.bi_ref
  249.3 0.7 slice.41.bi_ref
  250.0 0.7 slice.38.bi_ref
  250.7 2.3 finish.3.rest_0_
  253.0 2.3 finish.4.rest_0_
  255.5 0.5 copy-done.14
  256.1 0.1 copy-done.5
  256.2 0.1 copy-done.7
  256.3 2.3 finish.5
  (154 shorter events, 0.8 us)
Async XLA Ops:
  7.4 79.1 %collective-permute-start.13 = (bf16[4,272,256]{2,1,0:T(8,128)(2,1)}, bf16[4,272,256]{2,1,0:T(8,128)(2,1)S(1)}, u32[]{:S(2)}, u32[]{:S(2)}) collective-permute-start(bf16[4,272,256]{2,1,0:T(8,128)(2,1)} %get-tuple-element.77), channel_id=1, source_target_pairs={{1,0},{2,1},{3,2},{4,3},{5,4},{6,5},{7,6},{9,8},{10,9},{11,10},{12... | collective-permute-start | bytes 1671176 | tf_op jit(solution)/shard_map/ppermute | solution.py:427
  10.7 77.9 %collective-permute-start.12 = (bf16[4,272,256]{2,1,0:T(8,128)(2,1)}, bf16[4,272,256]{2,1,0:T(8,128)(2,1)S(1)}, u32[]{:S(2)}, u32[]{:S(2)}) collective-permute-start(bf16[4,272,256]{2,1,0:T(8,128)(2,1)} %get-tuple-element.76), channel_id=1, source_target_pairs={{0,1},{1,2},{2,3},{3,4},{4,5},{5,6},{6,7},{8,9},{9,10},{10,11},{11... | collective-permute-start | bytes 1671176 | tf_op jit(solution)/shard_map/ppermute | solution.py:427
  13.3 111.4 %collective-permute-start.14 = (bf16[2,272,256]{2,1,0:T(8,128)(2,1)}, bf16[2,272,256]{2,1,0:T(8,128)(2,1)}, u32[]{:S(2)}, u32[]{:S(2)}) collective-permute-start(bf16[2,272,256]{2,1,0:T(8,128)(2,1)} %get-tuple-element.78), channel_id=1, source_target_pairs={{0,120},{1,121},{2,122},{3,123},{4,124},{5,125},{6,126},{7,127},{8... | collective-permute-start | bytes 835592 | tf_op jit(solution)/shard_map/ppermute | solution.py:427
  20.6 72.7 %collective-permute-start.7 = (bf16[4,272,256]{2,1,0:T(8,128)(2,1)}, bf16[4,272,256]{2,1,0:T(8,128)(2,1)S(1)}, u32[]{:S(2)}, u32[]{:S(2)}) collective-permute-start(bf16[4,272,256]{2,1,0:T(8,128)(2,1)} %get-tuple-element.68), channel_id=1, source_target_pairs={{1,0},{2,1},{3,2},{4,3},{5,4},{6,5},{7,6},{9,8},{10,9},{11,10},{12... | collective-permute-start | bytes 1671176 | tf_op jit(solution)/shard_map/ppermute | solution.py:427
  23.9 71.5 %collective-permute-start.6 = (bf16[4,272,256]{2,1,0:T(8,128)(2,1)}, bf16[4,272,256]{2,1,0:T(8,128)(2,1)S(1)}, u32[]{:S(2)}, u32[]{:S(2)}) collective-permute-start(bf16[4,272,256]{2,1,0:T(8,128)(2,1)} %get-tuple-element.67), channel_id=1, source_target_pairs={{0,1},{1,2},{2,3},{3,4},{4,5},{5,6},{6,7},{8,9},{9,10},{10,11},{11... | collective-permute-start | bytes 1671176 | tf_op jit(solution)/shard_map/ppermute | solution.py:427
  67.4 19.1 %copy-start.41 = (bf16[1,272,256]{2,1,0:T(8,128)(2,1)S(1)}, bf16[1,272,256]{2,1,0:T(8,128)(2,1)}, u32[]{:S(2)}) copy-start(bf16[1,272,256]{2,1,0:T(8,128)(2,1)} %get-tuple-element.80) | copy-start | bytes 417796
  67.4 25.8 %copy-start.30 = (bf16[4,272,256]{2,1,0:T(8,128)(2,1)S(1)}, bf16[4,272,256]{2,1,0:T(8,128)(2,1)}, u32[]{:S(2)}) copy-start(bf16[4,272,256]{2,1,0:T(8,128)(2,1)} %get-tuple-element.59) | copy-start | bytes 1671172
  67.4 27.8 %copy-start = (bf16[2,272,256]{2,1,0:T(8,128)(2,1)S(1)}, bf16[2,272,256]{2,1,0:T(8,128)(2,1)}, u32[]{:S(2)}) copy-start(bf16[2,272,256]{2,1,0:T(8,128)(2,1)} %get-tuple-element.79) | copy-start | bytes 835588
  86.5 31.5 %collective-permute-start.16 = (bf16[1,272,256]{2,1,0:T(8,128)(2,1)S(1)}, bf16[1,272,256]{2,1,0:T(8,128)(2,1)S(1)}, u32[]{:S(2)}, u32[]{:S(2)}) collective-permute-start(bf16[1,272,256]{2,1,0:T(8,128)(2,1)S(1)} %copy-done.41), channel_id=1, source_target_pairs={{0,121},{1,122},{2,123},{3,124},{4,125},{5,126},{6,127},{8,17},{9,... | collective-permute-start | bytes 417800 | tf_op jit(solution)/shard_map/ppermute | solution.py:427
  88.6 18.0 %copy-start.40 = (bf16[1,272,256]{2,1,0:T(8,128)(2,1)S(1)}, bf16[1,272,256]{2,1,0:T(8,128)(2,1)}, u32[]{:S(2)}) copy-start(bf16[1,272,256]{2,1,0:T(8,128)(2,1)} %get-tuple-element.81) | copy-start | bytes 417796
  88.6 25.4 %copy-start.23 = (bf16[4,272,256]{2,1,0:T(8,128)(2,1)}, bf16[4,272,256]{2,1,0:T(8,128)(2,1)S(1)}, u32[]{:S(2)}) copy-start(bf16[4,272,256]{2,1,0:T(8,128)(2,1)S(1)} %collective-permute-done.12.col0_ref) | copy-start | bytes 1671172
  88.6 17.9 %collective-permute-start.1 = (bf16[4,272,256]{2,1,0:T(8,128)(2,1)}, bf16[4,272,256]{2,1,0:T(8,128)(2,1)S(1)}, u32[]{:S(2)}, u32[]{:S(2)}) collective-permute-start(bf16[4,272,256]{2,1,0:T(8,128)(2,1)} %get-tuple-element.60), channel_id=1, source_target_pairs={{1,0},{2,1},{3,2},{4,3},{5,4},{6,5},{7,6},{9,8},{10,9},{11,10},{12... | collective-permute-start | bytes 1671176 | tf_op jit(solution)/shard_map/ppermute | solution.py:427
  93.2 24.7 %copy-start.18 = (bf16[4,272,256]{2,1,0:T(8,128)(2,1)}, bf16[4,272,256]{2,1,0:T(8,128)(2,1)S(1)}, u32[]{:S(2)}) copy-start(bf16[4,272,256]{2,1,0:T(8,128)(2,1)S(1)} %collective-permute-done.7.col1_ref) | copy-start | bytes 1671172
  93.2 24.6 %collective-permute-start = (bf16[4,272,256]{2,1,0:T(8,128)(2,1)S(1)}, bf16[4,272,256]{2,1,0:T(8,128)(2,1)S(1)}, u32[]{:S(2)}, u32[]{:S(2)}) collective-permute-start(bf16[4,272,256]{2,1,0:T(8,128)(2,1)S(1)} %copy-done.30), channel_id=1, source_target_pairs={{0,1},{1,2},{2,3},{3,4},{4,5},{5,6},{6,7},{8,9},{9,10},{10,11},{11... | collective-permute-start | bytes 1671176 | tf_op jit(solution)/shard_map/ppermute | solution.py:427
  95.2 22.7 %copy-start.1 = (bf16[2,272,256]{2,1,0:T(8,128)(2,1)S(1)}, bf16[2,272,256]{2,1,0:T(8,128)(2,1)}, u32[]{:S(2)}) copy-start(bf16[2,272,256]{2,1,0:T(8,128)(2,1)} %get-tuple-element.62) | copy-start | bytes 835588
  95.3 22.7 %copy-start.33 = (bf16[2,272,256]{2,1,0:T(8,128)(2,1)S(1)}, bf16[2,272,256]{2,1,0:T(8,128)(2,1)}, u32[]{:S(2)}) copy-start(bf16[2,272,256]{2,1,0:T(8,128)(2,1)} %get-tuple-element.69) | copy-start | bytes 835588
  95.3 27.3 %copy-start.39 = (bf16[1,272,256]{2,1,0:T(8,128)(2,1)S(1)}, bf16[1,272,256]{2,1,0:T(8,128)(2,1)}, u32[]{:S(2)}) copy-start(bf16[1,272,256]{2,1,0:T(8,128)(2,1)} %get-tuple-element.71) | copy-start | bytes 417796
  95.3 29.4 %copy-start.38 = (bf16[1,272,256]{2,1,0:T(8,128)(2,1)S(1)}, bf16[1,272,256]{2,1,0:T(8,128)(2,1)}, u32[]{:S(2)}) copy-start(bf16[1,272,256]{2,1,0:T(8,128)(2,1)} %get-tuple-element.72) | copy-start | bytes 417796
  95.3 52.2 %copy-start.19 = (bf16[4,272,256]{2,1,0:T(8,128)(2,1)}, bf16[4,272,256]{2,1,0:T(8,128)(2,1)S(1)}, u32[]{:S(2)}) copy-start(bf16[4,272,256]{2,1,0:T(8,128)(2,1)S(1)} %collective-permute-done.6.col0_ref) | copy-start | bytes 1671172
  95.3 37.0 %collective-permute-start.15 = (bf16[4,272,256]{2,1,0:T(8,128)(2,1)S(1)}, bf16[4,272,256]{2,1,0:T(8,128)(2,1)S(1)}, u32[]{:S(2)}, u32[]{:S(2)}) collective-permute-start(bf16[4,272,256]{2,1,0:T(8,128)(2,1)S(1)} %pad_maximum_fusion.2), channel_id=1, source_target_pairs={{0,8},{1,9},{2,10},{3,11},{4,12},{5,13},{6,14},{7,15},{8,0},{9,1},... | collective-permute-start | bytes 1671176 | tf_op jit(solution)/shard_map/ppermute | solution.py:427
  106.6 41.0 %copy-start.20 = (bf16[4,272,256]{2,1,0:T(8,128)(2,1)}, bf16[4,272,256]{2,1,0:T(8,128)(2,1)S(1)}, u32[]{:S(2)}) copy-start(bf16[4,272,256]{2,1,0:T(8,128)(2,1)S(1)} %collective-permute-done.1.col1_ref) | copy-start | bytes 1671172
  106.6 16.0 %collective-permute-start.17 = (bf16[1,272,256]{2,1,0:T(8,128)(2,1)S(1)}, bf16[1,272,256]{2,1,0:T(8,128)(2,1)S(1)}, u32[]{:S(2)}, u32[]{:S(2)}) collective-permute-start(bf16[1,272,256]{2,1,0:T(8,128)(2,1)S(1)} %copy-done.40), channel_id=1, source_target_pairs={{1,120},{2,121},{3,122},{4,123},{5,124},{6,125},{7,126},{9,16},{10... | collective-permute-start | bytes 417800 | tf_op jit(solution)/shard_map/ppermute | solution.py:427
  117.9 29.7 %copy-start.21 = (bf16[4,272,256]{2,1,0:T(8,128)(2,1)}, bf16[4,272,256]{2,1,0:T(8,128)(2,1)S(1)}, u32[]{:S(2)}) copy-start(bf16[4,272,256]{2,1,0:T(8,128)(2,1)S(1)} %collective-permute-done.col0_ref) | copy-start | bytes 1671172
  117.9 39.7 %collective-permute-start.9 = (bf16[4,272,256]{2,1,0:T(8,128)(2,1)S(1)}, bf16[4,272,256]{2,1,0:T(8,128)(2,1)S(1)}, u32[]{:S(2)}, u32[]{:S(2)}) collective-permute-start(bf16[4,272,256]{2,1,0:T(8,128)(2,1)S(1)} %pad_maximum_fusion.1), channel_id=1, source_target_pairs={{0,8},{1,9},{2,10},{3,11},{4,12},{5,13},{6,14},{7,15},{8,0},{9,1},... | collective-permute-start | bytes 1671176 | tf_op jit(solution)/shard_map/ppermute | solution.py:427
  118.0 34.6 %collective-permute-start.8 = (bf16[2,272,256]{2,1,0:T(8,128)(2,1)S(1)}, bf16[2,272,256]{2,1,0:T(8,128)(2,1)S(1)}, u32[]{:S(2)}, u32[]{:S(2)}) collective-permute-start(bf16[2,272,256]{2,1,0:T(8,128)(2,1)S(1)} %copy-done.33), channel_id=1, source_target_pairs={{0,120},{1,121},{2,122},{3,123},{4,124},{5,125},{6,126},{7,127},{8... | collective-permute-start | bytes 835592 | tf_op jit(solution)/shard_map/ppermute | solution.py:427
  122.6 25.0 %collective-permute-start.10 = (bf16[1,272,256]{2,1,0:T(8,128)(2,1)S(1)}, bf16[1,272,256]{2,1,0:T(8,128)(2,1)S(1)}, u32[]{:S(2)}, u32[]{:S(2)}) collective-permute-start(bf16[1,272,256]{2,1,0:T(8,128)(2,1)S(1)} %copy-done.39), channel_id=1, source_target_pairs={{0,121},{1,122},{2,123},{3,124},{4,125},{5,126},{6,127},{8,17},{9,... | collective-permute-start | bytes 417800 | tf_op jit(solution)/shard_map/ppermute | solution.py:427
  124.7 22.9 %collective-permute-start.11 = (bf16[1,272,256]{2,1,0:T(8,128)(2,1)S(1)}, bf16[1,272,256]{2,1,0:T(8,128)(2,1)S(1)}, u32[]{:S(2)}, u32[]{:S(2)}) collective-permute-start(bf16[1,272,256]{2,1,0:T(8,128)(2,1)S(1)} %copy-done.38), channel_id=1, source_target_pairs={{1,120},{2,121},{3,122},{4,123},{5,124},{6,125},{7,126},{9,16},{10... | collective-permute-start | bytes 417800 | tf_op jit(solution)/shard_map/ppermute | solution.py:427
  132.4 54.4 %collective-permute-start.3 = (bf16[4,272,256]{2,1,0:T(8,128)(2,1)S(1)}, bf16[4,272,256]{2,1,0:T(8,128)(2,1)S(1)}, u32[]{:S(2)}, u32[]{:S(2)}) collective-permute-start(bf16[4,272,256]{2,1,0:T(8,128)(2,1)S(1)} %pad_maximum_fusion), channel_id=1, source_target_pairs={{0,8},{1,9},{2,10},{3,11},{4,12},{5,13},{6,14},{7,15},{8,0},{9,1},... | collective-permute-start | bytes 1671176 | tf_op jit(solution)/shard_map/ppermute | solution.py:427
  133.2 19.5 %copy-start.36 = (bf16[1,272,256]{2,1,0:T(8,128)(2,1)S(1)}, bf16[1,272,256]{2,1,0:T(8,128)(2,1)}, u32[]{:S(2)}) copy-start(bf16[1,272,256]{2,1,0:T(8,128)(2,1)} %get-tuple-element.64) | copy-start | bytes 417796
  147.6 31.3 %collective-permute-start.2 = (bf16[2,272,256]{2,1,0:T(8,128)(2,1)S(1)}, bf16[2,272,256]{2,1,0:T(8,128)(2,1)S(1)}, u32[]{:S(2)}, u32[]{:S(2)}) collective-permute-start(bf16[2,272,256]{2,1,0:T(8,128)(2,1)S(1)} %copy-done.32), channel_id=1, source_target_pairs={{0,120},{1,121},{2,122},{3,123},{4,124},{5,125},{6,126},{7,127},{8... | collective-permute-start | bytes 835592 | tf_op jit(solution)/shard_map/ppermute | solution.py:427
  147.7 25.1 %collective-permute-start.4 = (bf16[1,272,256]{2,1,0:T(8,128)(2,1)S(1)}, bf16[1,272,256]{2,1,0:T(8,128)(2,1)S(1)}, u32[]{:S(2)}, u32[]{:S(2)}) collective-permute-start(bf16[1,272,256]{2,1,0:T(8,128)(2,1)S(1)} %copy-done.37), channel_id=1, source_target_pairs={{0,121},{1,122},{2,123},{3,124},{4,125},{5,126},{6,127},{8,17},{9,... | collective-permute-start | bytes 417800 | tf_op jit(solution)/shard_map/ppermute | solution.py:427
  152.7 24.3 %collective-permute-start.5 = (bf16[1,272,256]{2,1,0:T(8,128)(2,1)S(1)}, bf16[1,272,256]{2,1,0:T(8,128)(2,1)S(1)}, u32[]{:S(2)}, u32[]{:S(2)}) collective-permute-start(bf16[1,272,256]{2,1,0:T(8,128)(2,1)S(1)} %copy-done.36), channel_id=1, source_target_pairs={{1,120},{2,121},{3,122},{4,123},{5,124},{6,125},{7,126},{9,16},{10... | collective-permute-start | bytes 417800 | tf_op jit(solution)/shard_map/ppermute | solution.py:427
  157.6 44.5 %collective-permute-start.30 = (bf16[4,128,256]{2,1,0:T(8,128)(2,1)}, bf16[4,128,256]{2,1,0:T(8,128)(2,1)S(1)}, u32[]{:S(2)}, u32[]{:S(2)}) collective-permute-start(bf16[4,128,256]{2,1,0:T(8,128)(2,1)} %get-tuple-element.104), channel_id=1, source_target_pairs={{0,8},{1,9},{2,10},{3,11},{4,12},{5,13},{6,14},{7,15},{8,0},{9,1},... | collective-permute-start | bytes 786440 | tf_op jit(solution)/shard_map/ppermute | solution.py:427
  158.4 18.6 %copy-start.51 = (bf16[1,128,256]{2,1,0:T(8,128)(2,1)S(1)}, bf16[1,128,256]{2,1,0:T(8,128)(2,1)}, u32[]{:S(2)}) copy-start(bf16[1,128,256]{2,1,0:T(8,128)(2,1)} %get-tuple-element.107) | copy-start | bytes 196612
  158.4 20.5 %copy-start.50 = (bf16[1,128,256]{2,1,0:T(8,128)(2,1)S(1)}, bf16[1,128,256]{2,1,0:T(8,128)(2,1)}, u32[]{:S(2)}) copy-start(bf16[1,128,256]{2,1,0:T(8,128)(2,1)} %get-tuple-element.108) | copy-start | bytes 196612
  172.8 46.3 %collective-permute-start.33 = (bf16[2,128,256]{2,1,0:T(8,128)(2,1)S(1)}, bf16[2,128,256]{2,1,0:T(8,128)(2,1)S(1)}, u32[]{:S(2)}, u32[]{:S(2)}) collective-permute-start(bf16[2,128,256]{2,1,0:T(8,128)(2,1)S(1)} %copy-done.48), channel_id=1, source_target_pairs={{0,120},{1,121},{2,122},{3,123},{4,124},{5,125},{6,126},{7,127},{8... | collective-permute-start | bytes 393224 | tf_op jit(solution)/shard_map/ppermute | solution.py:427
  177.0 25.3 %collective-permute-start.34 = (bf16[1,128,256]{2,1,0:T(8,128)(2,1)S(1)}, bf16[1,128,256]{2,1,0:T(8,128)(2,1)S(1)}, u32[]{:S(2)}, u32[]{:S(2)}) collective-permute-start(bf16[1,128,256]{2,1,0:T(8,128)(2,1)S(1)} %copy-done.51), channel_id=1, source_target_pairs={{0,121},{1,122},{2,123},{3,124},{4,125},{5,126},{6,127},{8,17},{9,... | collective-permute-start | bytes 196616 | tf_op jit(solution)/shard_map/ppermute | solution.py:427
  178.9 25.3 %collective-permute-start.35 = (bf16[1,128,256]{2,1,0:T(8,128)(2,1)S(1)}, bf16[1,128,256]{2,1,0:T(8,128)(2,1)S(1)}, u32[]{:S(2)}, u32[]{:S(2)}) collective-permute-start(bf16[1,128,256]{2,1,0:T(8,128)(2,1)S(1)} %copy-done.50), channel_id=1, source_target_pairs={{1,120},{2,121},{3,122},{4,123},{5,124},{6,125},{7,126},{9,16},{10... | collective-permute-start | bytes 196616 | tf_op jit(solution)/shard_map/ppermute | solution.py:427
  186.8 25.3 %collective-permute-start.24 = (bf16[4,128,256]{2,1,0:T(8,128)(2,1)}, bf16[4,128,256]{2,1,0:T(8,128)(2,1)S(1)}, u32[]{:S(2)}, u32[]{:S(2)}) collective-permute-start(bf16[4,128,256]{2,1,0:T(8,128)(2,1)} %get-tuple-element.97), channel_id=1, source_target_pairs={{0,8},{1,9},{2,10},{3,11},{4,12},{5,13},{6,14},{7,15},{8,0},{9,1},... | collective-permute-start | bytes 786440 | tf_op jit(solution)/shard_map/ppermute | solution.py:427
  187.6 16.6 %copy-start.52 = (bf16[1,128,256]{2,1,0:T(8,128)(2,1)S(1)}, bf16[1,128,256]{2,1,0:T(8,128)(2,1)}, u32[]{:S(2)}) copy-start(bf16[1,128,256]{2,1,0:T(8,128)(2,1)} %get-tuple-element.101) | copy-start | bytes 196612
  187.6 26.4 %copy-start.26 = (bf16[4,128,256]{2,1,0:T(8,128)(2,1)S(1)}, bf16[4,128,256]{2,1,0:T(8,128)(2,1)}, u32[]{:S(2)}) copy-start(bf16[4,128,256]{2,1,0:T(8,128)(2,1)} %get-tuple-element.98) | copy-start | bytes 786436
  187.6 26.4 %copy-start.27 = (bf16[4,128,256]{2,1,0:T(8,128)(2,1)S(1)}, bf16[4,128,256]{2,1,0:T(8,128)(2,1)}, u32[]{:S(2)}) copy-start(bf16[4,128,256]{2,1,0:T(8,128)(2,1)} %get-tuple-element.96) | copy-start | bytes 786436
  187.6 26.5 %copy-start.49 = (bf16[2,128,256]{2,1,0:T(8,128)(2,1)S(1)}, bf16[2,128,256]{2,1,0:T(8,128)(2,1)}, u32[]{:S(2)}) copy-start(bf16[2,128,256]{2,1,0:T(8,128)(2,1)} %get-tuple-element.99) | copy-start | bytes 393220
  202.1 18.9 %collective-permute-start.18 = (bf16[4,128,256]{2,1,0:T(8,128)(2,1)}, bf16[4,128,256]{2,1,0:T(8,128)(2,1)S(1)}, u32[]{:S(2)}, u32[]{:S(2)}) collective-permute-start(bf16[4,128,256]{2,1,0:T(8,128)(2,1)} %get-tuple-element.90), channel_id=1, source_target_pairs={{0,8},{1,9},{2,10},{3,11},{4,12},{5,13},{6,14},{7,15},{8,0},{9,1},... | collective-permute-start | bytes 786440 | tf_op jit(solution)/shard_map/ppermute | solution.py:427
  202.3 48.4 %copy-start.16 = (bf16[1,128,256]{2,1,0:T(8,128)(2,1)}, bf16[1,128,256]{2,1,0:T(8,128)(2,1)S(1)}, u32[]{:S(2)}) copy-start(bf16[1,128,256]{2,1,0:T(8,128)(2,1)S(1)} %collective-permute-done.34.bg0_ref) | copy-start | bytes 196612
  202.3 11.8 %collective-permute-start.28 = (bf16[1,128,256]{2,1,0:T(8,128)(2,1)S(1)}, bf16[1,128,256]{2,1,0:T(8,128)(2,1)S(1)}, u32[]{:S(2)}, u32[]{:S(2)}) collective-permute-start(bf16[1,128,256]{2,1,0:T(8,128)(2,1)S(1)} %copy-done.53), channel_id=1, source_target_pairs={{0,121},{1,122},{2,123},{3,124},{4,125},{5,126},{6,127},{8,17},{9,... | collective-permute-start | bytes 196616 | tf_op jit(solution)/shard_map/ppermute | solution.py:427
  204.2 46.4 %copy-start.17 = (bf16[1,128,256]{2,1,0:T(8,128)(2,1)}, bf16[1,128,256]{2,1,0:T(8,128)(2,1)S(1)}, u32[]{:S(2)}) copy-start(bf16[1,128,256]{2,1,0:T(8,128)(2,1)S(1)} %collective-permute-done.35.bg1_ref) | copy-start | bytes 196612
  204.2 10.3 %collective-permute-start.29 = (bf16[1,128,256]{2,1,0:T(8,128)(2,1)S(1)}, bf16[1,128,256]{2,1,0:T(8,128)(2,1)S(1)}, u32[]{:S(2)}, u32[]{:S(2)}) collective-permute-start(bf16[1,128,256]{2,1,0:T(8,128)(2,1)S(1)} %copy-done.52), channel_id=1, source_target_pairs={{1,120},{2,121},{3,122},{4,123},{5,124},{6,125},{7,126},{9,16},{10... | collective-permute-start | bytes 196616 | tf_op jit(solution)/shard_map/ppermute | solution.py:427
  212.1 17.2 %collective-permute-start.31 = (bf16[4,128,256]{2,1,0:T(8,128)(2,1)S(1)}, bf16[4,128,256]{2,1,0:T(8,128)(2,1)S(1)}, u32[]{:S(2)}, u32[]{:S(2)}) collective-permute-start(bf16[4,128,256]{2,1,0:T(8,128)(2,1)S(1)} %get-tuple-element.112), channel_id=1, source_target_pairs={{0,1},{1,2},{2,3},{3,4},{4,5},{5,6},{6,7},{8,9},{9,10},{10,11},{11... | collective-permute-start | bytes 786440 | tf_op jit(solution)/shard_map/ppermute | solution.py:427
  214.1 38.9 %copy-start.12 = (bf16[1,128,256]{2,1,0:T(8,128)(2,1)}, bf16[1,128,256]{2,1,0:T(8,128)(2,1)S(1)}, u32[]{:S(2)}) copy-start(bf16[1,128,256]{2,1,0:T(8,128)(2,1)S(1)} %collective-permute-done.28.bg0_ref) | copy-start | bytes 196612
  214.1 13.3 %collective-permute-start.27 = (bf16[2,128,256]{2,1,0:T(8,128)(2,1)S(1)}, bf16[2,128,256]{2,1,0:T(8,128)(2,1)S(1)}, u32[]{:S(2)}, u32[]{:S(2)}) collective-permute-start(bf16[2,128,256]{2,1,0:T(8,128)(2,1)S(1)} %copy-done.49), channel_id=1, source_target_pairs={{0,120},{1,121},{2,122},{3,123},{4,124},{5,125},{6,126},{7,127},{8... | collective-permute-start | bytes 393224 | tf_op jit(solution)/shard_map/ppermute | solution.py:427
  214.5 38.5 %copy-start.13 = (bf16[1,128,256]{2,1,0:T(8,128)(2,1)}, bf16[1,128,256]{2,1,0:T(8,128)(2,1)S(1)}, u32[]{:S(2)}) copy-start(bf16[1,128,256]{2,1,0:T(8,128)(2,1)S(1)} %collective-permute-done.29.bg1_ref) | copy-start | bytes 196612
  214.5 19.7 %collective-permute-start.32 = (bf16[4,128,256]{2,1,0:T(8,128)(2,1)S(1)}, bf16[4,128,256]{2,1,0:T(8,128)(2,1)S(1)}, u32[]{:S(2)}, u32[]{:S(2)}) collective-permute-start(bf16[4,128,256]{2,1,0:T(8,128)(2,1)S(1)} %get-tuple-element.111), channel_id=1, source_target_pairs={{1,0},{2,1},{3,2},{4,3},{5,4},{6,5},{7,6},{9,8},{10,9},{11,10},{12... | collective-permute-start | bytes 786440 | tf_op jit(solution)/shard_map/ppermute | solution.py:427
  219.1 31.5 %copy-start.9 = (bf16[2,128,256]{2,1,0:T(8,128)(2,1)}, bf16[2,128,256]{2,1,0:T(8,128)(2,1)S(1)}, u32[]{:S(2)}) copy-start(bf16[2,128,256]{2,1,0:T(8,128)(2,1)S(1)} %collective-permute-done.33.bo_ref) | copy-start | bytes 393220
  219.1 19.7 %collective-permute-start.25 = (bf16[4,128,256]{2,1,0:T(8,128)(2,1)S(1)}, bf16[4,128,256]{2,1,0:T(8,128)(2,1)S(1)}, u32[]{:S(2)}, u32[]{:S(2)}) collective-permute-start(bf16[4,128,256]{2,1,0:T(8,128)(2,1)S(1)} %get-tuple-element.114), channel_id=1, source_target_pairs={{0,1},{1,2},{2,3},{3,4},{4,5},{5,6},{6,7},{8,9},{9,10},{10,11},{11... | collective-permute-start | bytes 786440 | tf_op jit(solution)/shard_map/ppermute | solution.py:427
  221.0 19.8 %collective-permute-start.26 = (bf16[4,128,256]{2,1,0:T(8,128)(2,1)S(1)}, bf16[4,128,256]{2,1,0:T(8,128)(2,1)S(1)}, u32[]{:S(2)}, u32[]{:S(2)}) collective-permute-start(bf16[4,128,256]{2,1,0:T(8,128)(2,1)S(1)} %get-tuple-element.113), channel_id=1, source_target_pairs={{1,0},{2,1},{3,2},{4,3},{5,4},{6,5},{7,6},{9,8},{10,9},{11,10},{12... | collective-permute-start | bytes 786440 | tf_op jit(solution)/shard_map/ppermute | solution.py:427
  227.4 25.6 %copy-start.10 = (bf16[2,128,256]{2,1,0:T(8,128)(2,1)}, bf16[2,128,256]{2,1,0:T(8,128)(2,1)S(1)}, u32[]{:S(2)}) copy-start(bf16[2,128,256]{2,1,0:T(8,128)(2,1)S(1)} %collective-permute-done.27.bo_ref) | copy-start | bytes 393220
  227.4 28.0 %collective-permute-start.19 = (bf16[4,128,256]{2,1,0:T(8,128)(2,1)}, bf16[4,128,256]{2,1,0:T(8,128)(2,1)S(1)}, u32[]{:S(2)}, u32[]{:S(2)}) collective-permute-start(bf16[4,128,256]{2,1,0:T(8,128)(2,1)} %get-tuple-element.116), channel_id=1, source_target_pairs={{0,1},{1,2},{2,3},{3,4},{4,5},{5,6},{6,7},{8,9},{9,10},{10,11},{11... | collective-permute-start | bytes 786440 | tf_op jit(solution)/shard_map/ppermute | solution.py:427
  229.4 21.3 %copy-start.3 = (bf16[4,128,256]{2,1,0:T(8,128)(2,1)}, bf16[4,128,256]{2,1,0:T(8,128)(2,1)S(1)}, u32[]{:S(2)}) copy-start(bf16[4,128,256]{2,1,0:T(8,128)(2,1)S(1)} %collective-permute-done.31.b0_ref) | copy-start | bytes 786436
  229.4 26.1 %collective-permute-start.20 = (bf16[4,128,256]{2,1,0:T(8,128)(2,1)}, bf16[4,128,256]{2,1,0:T(8,128)(2,1)S(1)}, u32[]{:S(2)}, u32[]{:S(2)}) collective-permute-start(bf16[4,128,256]{2,1,0:T(8,128)(2,1)} %get-tuple-element.115), channel_id=1, source_target_pairs={{1,0},{2,1},{3,2},{4,3},{5,4},{6,5},{7,6},{9,8},{10,9},{11,10},{12... | collective-permute-start | bytes 786440 | tf_op jit(solution)/shard_map/ppermute | solution.py:427
  234.2 16.4 %copy-start.4 = (bf16[4,128,256]{2,1,0:T(8,128)(2,1)}, bf16[4,128,256]{2,1,0:T(8,128)(2,1)S(1)}, u32[]{:S(2)}) copy-start(bf16[4,128,256]{2,1,0:T(8,128)(2,1)S(1)} %collective-permute-done.32.b1_ref) | copy-start | bytes 786436
  234.2 21.2 %collective-permute-start.21 = (bf16[2,128,256]{2,1,0:T(8,128)(2,1)}, bf16[2,128,256]{2,1,0:T(8,128)(2,1)S(1)}, u32[]{:S(2)}, u32[]{:S(2)}) collective-permute-start(bf16[2,128,256]{2,1,0:T(8,128)(2,1)} %get-tuple-element.92), channel_id=1, source_target_pairs={{0,120},{1,121},{2,122},{3,123},{4,124},{5,125},{6,126},{7,127},{8... | collective-permute-start | bytes 393224 | tf_op jit(solution)/shard_map/ppermute | solution.py:427
  238.8 16.6 %collective-permute-start.22 = (bf16[1,128,256]{2,1,0:T(8,128)(2,1)}, bf16[1,128,256]{2,1,0:T(8,128)(2,1)S(1)}, u32[]{:S(2)}, u32[]{:S(2)}) collective-permute-start(bf16[1,128,256]{2,1,0:T(8,128)(2,1)} %get-tuple-element.93), channel_id=1, source_target_pairs={{0,121},{1,122},{2,123},{3,124},{4,125},{5,126},{6,127},{8,17},{9,... | collective-permute-start | bytes 196616 | tf_op jit(solution)/shard_map/ppermute | solution.py:427
  240.9 14.5 %collective-permute-start.23 = (bf16[1,128,256]{2,1,0:T(8,128)(2,1)}, bf16[1,128,256]{2,1,0:T(8,128)(2,1)S(1)}, u32[]{:S(2)}, u32[]{:S(2)}) collective-permute-start(bf16[1,128,256]{2,1,0:T(8,128)(2,1)} %get-tuple-element.94), channel_id=1, source_target_pairs={{1,120},{2,121},{3,122},{4,123},{5,124},{6,125},{7,126},{9,16},{10... | collective-permute-start | bytes 196616 | tf_op jit(solution)/shard_map/ppermute | solution.py:427
  (26 other events, 219.1 us)
